TPU v7x, 256 devices: a whole 4x4x8 slice. The times are simulated.
256 devices in a mesh: ctx: 32 (over z, x_hi, core), head: 8 (over y, x_lo).
Axes of the slice: x: 4 (x_hi: 2, x_lo: 2; x = x_hi * 2 + x_lo), y: 4, z: 8, core: 2. Of those that a mesh axis runs over, the one named last changes fastest.
Arguments:
- queries: bfloat16 [4096, 6144], P('ctx', 'head'), may hold values from -6 to 6
- key_states: bfloat16 [4096, 1024], P('ctx', 'head'), may hold values from -8 to 8
- value_states: bfloat16 [4096, 1024], P('ctx', 'head'), may hold values from -6 to 6
- out_grad: bfloat16 [4096, 6144], P('ctx', 'head'), may hold values from -6 to 6
- norm_gain: float32 [6144], P('head'), may hold values from 0.1 to 1.9
- mask_kind: int32 [8], replicated, may hold values from 0 to 1
- range_start: int32 [8], replicated, may hold values from 0 to 7, as said below
- placement: int32 [8], replicated, may hold values from 0 to 7, each once
Outputs:
- attn_out: bfloat16 [4096, 6144], P('ctx', 'head')
- d_queries: bfloat16 [4096, 6144], P('ctx', 'head')
- d_keys: bfloat16 [4096, 1024], P('ctx', 'head')
- d_values: bfloat16 [4096, 1024], P('ctx', 'head')
Inputs may be any that keep to these rules, and one draw needn't show every extreme that they name: range_start[i] <= i for every span i; the last span sees no earlier span. `placement`: every span number appears in exactly one slot.
All inputs are finite; a program needn't handle non-finite values.
Results may differ from a plain program's by a relative error of at most 0.04.
Values may be sent and summed in bfloat16 or wider, within the bound.
No kernel may reach another device: no remote copies, remote signals or barrier semaphores. Data moves between devices by JAX's collectives and lax.ppermute only.
A program may use at most 64 MiB of HBM per device.

v0:
```python
import functools
import math

import jax
import jax.numpy as jnp
from jax import lax
from jax.experimental import pallas as pl
from jax.experimental.pallas import tpu as pltpu
from jax.sharding import Mesh
from jax.sharding import PartitionSpec as P

NEG = -1e30
EPS = 1e-06
LOG2E = 1.4426950408889634
LN2 = 0.6931471805599453
LANES = 128
STATS = 3

CTX = ("z", "xh", "core")
HEAD = ("y", "xl")
SWAP = [(0, 1), (1, 0)]
VMEM_LIMIT = 48 * 2**20
SMALL_LIMIT = 8 * 2**20
LONG = pl.CostEstimate(flops=2 * 10**10, bytes_accessed=2**20, transcendentals=0)
SHORT = pl.CostEstimate(flops=2**10, bytes_accessed=2**10, transcendentals=0)


def dot_rows(left_side, right_side):
    return lax.dot_general(
        left_side, right_side, (((1,), (1,)), ((), ())), preferred_element_type=jnp.float32
    )


def dot_cols(left_side, right_side):
    return lax.dot_general(
        left_side, right_side, (((0,), (0,)), ((), ())), preferred_element_type=jnp.float32
    )


def dot(left_side, right_side):
    return jnp.dot(left_side, right_side, preferred_element_type=jnp.float32)


def lane_tiles(x):
    return [x[:, j : j + LANES] for j in range(0, x.shape[1], LANES)]


def lane_sum(x):
    return jnp.sum(x, axis=1, keepdims=True)


def unpack(plan, spans):
    own_span = plan[3 + 2 * spans + plan[0]]
    lower = plan[3 + spans + own_span]
    return own_span - lower + 1, lower, own_span


def visible_slots(plan, order, spans):
    count, lower, own_span = unpack(plan, spans)

    @pl.loop(0, spans)
    def _(slot):
        span = plan[3 + 2 * spans + slot]

        @pl.when((lower <= span) & (span < own_span))
        def _():
            order[span - lower + 1] = slot

    order[0] = plan[0]

    return count, own_span


def stacked(order, first, n, lanes, kv_mine, kv_mate):
    parts = []
    for k in range(n):
        slot = order[first + k]
        parts += [kv_mine[slot, :, lanes], kv_mate[slot, :, lanes]]
    return jnp.concatenate(parts, axis=0)


def by_pairs(count, body):
    @pl.loop(0, count // 2)
    def _(i):
        body(2 * i, 2)

    @pl.when(count % 2 == 1)
    def _():
        body(count - 1, 1)


def columns_of(table):
    pad = jnp.zeros((LANES - table.shape[0], LANES), jnp.float32)
    return jnp.transpose(jnp.concatenate([table, pad], axis=0))


def row_squares(queries, q_mate, parts):
    for side, rows_of in enumerate((queries, q_mate)):
        wide = rows_of[...].astype(jnp.float32)
        total = functools.reduce(jnp.add, lane_tiles(wide * wide))
        parts[side : side + 1, :] = jnp.sum(jnp.transpose(total), axis=0, keepdims=True)


def prepare(queries, q_mate, out_grad, g_mate, q_raw, g_raw, *, tok, heads, dim):
    for side, (q_part, g_part) in enumerate(((queries, out_grad), (q_mate, g_mate))):
        for h in range(heads):
            first = (side * heads + h) * tok
            q_raw[first : first + tok, :] = q_part[:, h * dim : (h + 1) * dim]
            g_raw[first : first + tok, :] = g_part[:, h * dim : (h + 1) * dim]


def merge(out_keep, out_got, dq_keep, dq_got, out, dq):
    out[...] = (out_keep[...].astype(jnp.float32) + out_got[...].astype(jnp.float32)).astype(out.dtype)
    dq[...] = (dq_keep[...].astype(jnp.float32) + dq_got[...].astype(jnp.float32)).astype(dq.dtype)


def forward(
    plan, square_sum, gain, q_raw, g_raw, kv_mine, kv_mate,
    prob_out, acc, stats, q_rows,
    order, score, prob, row_max, row_sum, sems,
    *, tok, heads, dim, group, width,
):
    spans = order.shape[0]
    half = heads * tok
    keys_n = 2 * tok
    sums = columns_of(square_sum[...])
    scale = lax.rsqrt(sums / width + EPS) * (LOG2E / math.sqrt(dim))
    for side in range(2):
        for h in range(heads):
            r = slice(side * half + h * tok, side * half + (h + 1) * tok)
            normed = q_raw[r, :].astype(jnp.float32) * scale[:, side : side + 1]
            normed = normed * gain[:, h * dim : (h + 1) * dim]
            q_rows[r, :] = normed.astype(jnp.bfloat16)
    count, own_span = visible_slots(plan, order, spans)
    row_max[...] = jnp.full_like(row_max, NEG)
    row_sum[...] = jnp.zeros_like(row_sum)
    acc[...] = jnp.zeros_like(acc)
    chunks = [slice(r, r + group) for r in range(0, 2 * half, group)]

    def score_block(i, masked):
        slot = order[i]
        keys = jnp.concatenate([kv_mine[slot, :, :dim], kv_mate[slot, :, :dim]], axis=0)
        if masked:
            free = plan[3 + own_span] == 0
            q_t = lax.broadcasted_iota(jnp.int32, (group, keys_n), 0) % tok
            k_t = lax.broadcasted_iota(jnp.int32, (group, keys_n), 1)
            core = plan[2]
            k_pos = plan[1] * keys_n + jnp.where(
                k_t < tok, core * tok + k_t, (1 - core) * tok + k_t - tok
            )
        for c in chunks:
            s = dot_rows(q_rows[c, :], keys)
            if masked:
                q_xh = plan[1] if c.start < half else 1 - plan[1]
                q_pos = (q_xh * 2 + core) * tok + q_t
                s = jnp.where((k_pos <= q_pos) | free, s, NEG)
            score[i, c, :] = s
            row_max[c, :] = functools.reduce(jnp.maximum, lane_tiles(s), row_max[c, :])

    score_block(0, True)

    def score_blocks(first, n):
        keys = stacked(order, first, n, slice(0, dim), kv_mine, kv_mate)
        for c in chunks:
            s = dot_rows(q_rows[c, :], keys)
            for k in range(n):
                score[first + k, c, :] = s[:, k * keys_n : (k + 1) * keys_n]
            row_max[c, :] = functools.reduce(jnp.maximum, lane_tiles(s), row_max[c, :])

    by_pairs(count - 1, lambda first, n: score_blocks(first + 1, n))

    for c in chunks:
        top = jnp.max(row_max[c, :], axis=1, keepdims=True)
        row_max[c, :] = jnp.broadcast_to(top, (group, LANES))

    def weigh(first, n):
        values = stacked(order, first, n, slice(dim, 2 * dim), kv_mine, kv_mate)
        for c in chunks:
            top = row_max[c, :]
            blocks = [lane_tiles(score[first + k, c, :]) for k in range(n)]
            tiles = [[jnp.exp2(t - top) for t in b] for b in blocks]
            row_sum[c, :] += functools.reduce(jnp.add, sum(tiles, []))
            p = [jnp.concatenate(b, axis=1).astype(jnp.bfloat16) for b in tiles]
            for k in range(n):
                prob[first + k, c, :] = p[k]
            acc[c, :] += dot(jnp.concatenate(p, axis=1), values)
        for k in range(n):
            b = first + k
            pltpu.make_async_copy(prob.at[b], prob_out.at[b], sems.at[b]).start()

    by_pairs(count, weigh)

    lane = lax.broadcasted_iota(jnp.int32, (tok, LANES), 1)
    table = jnp.zeros((tok, LANES), jnp.float32)
    for j in range(2 * heads):
        r = slice(j * tok, (j + 1) * tok)
        grad = g_raw[r, :].astype(jnp.float32)
        table = jnp.where(lane == STATS * j, row_max[r, :], table)
        table = jnp.where(lane == STATS * j + 1, lane_sum(row_sum[r, :]), table)
        table = jnp.where(lane == STATS * j + 2, lane_sum(grad * acc[r, :]), table)
    stats[...] = jnp.transpose(table)[: stats.shape[0], :]

    @pl.loop(0, count)
    def _(b):
        pltpu.make_async_copy(prob.at[b], prob_out.at[b], sems.at[b]).wait()


def backward(
    plan, prob_in, stats_own, stats_mate, acc_in, q_rows, g_raw, kv_mine, kv_mate,
    out_keep, out_give, ds_out, dkv_keep, dkv_give,
    order, g_rows, prob, ds_rows, delta_rows, q_cols, g_cols, in_sems, sems,
    *, tok, heads, dim, group,
):
    spans = order.shape[0]
    count, _ = visible_slots(plan, order, spans)

    @pl.loop(0, count)
    def _(b):
        pltpu.make_async_copy(prob_in.at[b], prob.at[b], in_sems.at[b]).start()

    half = heads * tok
    mine, theirs = columns_of(stats_own[...]), columns_of(stats_mate[...])
    for j in range(2 * heads):
        r = slice(j * tok, (j + 1) * tok)
        h = slice((j % heads) * dim, (j % heads + 1) * dim)
        a, b = STATS * j, STATS * ((j + heads) % (2 * heads))
        top = jnp.maximum(mine[:, a : a + 1], theirs[:, b : b + 1])
        f_mine = jnp.exp2(mine[:, a : a + 1] - top)
        f_theirs = jnp.exp2(theirs[:, b : b + 1] - top)
        total = mine[:, a + 1 : a + 2] * f_mine + theirs[:, b + 1 : b + 2] * f_theirs
        scale = f_mine / total
        delta = (mine[:, a + 2 : a + 3] * f_mine + theirs[:, b + 2 : b + 3] * f_theirs) / total
        delta_rows[r, :] = jnp.broadcast_to(delta * scale, (tok, LANES))
        out = out_keep if j < heads else out_give
        g_rows[r, :] = (g_raw[r, :].astype(jnp.float32) * scale).astype(jnp.bfloat16)
        out[:, h] = (acc_in[r, :] * scale).astype(jnp.bfloat16)
    for j in range(2 * heads):
        r = slice(j * tok, (j + 1) * tok)
        q_cols[:, r] = jnp.transpose(q_rows[r, :])
        g_cols[:, r] = jnp.transpose(g_rows[r, :])
    chunks = [slice(r, r + group) for r in range(0, 2 * half, group)]

    _, lower, own_span = unpack(plan, spans)

    @pl.loop(0, spans)
    def _(slot):
        span = plan[3 + 2 * spans + slot]

        @pl.when((span < lower) | (span > own_span))
        def _():
            dkv_keep[slot] = jnp.zeros(dkv_keep.shape[1:], dkv_keep.dtype)
            dkv_give[slot] = jnp.zeros(dkv_give.shape[1:], dkv_give.dtype)

    def grads_of(first, n):
        values = stacked(order, first, n, slice(dim, 2 * dim), kv_mine, kv_mate)
        for k in range(n):
            b = first + k
            pltpu.make_async_copy(prob_in.at[b], prob.at[b], in_sems.at[b]).wait()
        for c in chunks:
            d_prob = lane_tiles(dot_rows(g_rows[c, :], values))
            delta = delta_rows[c, :]
            p = sum([lane_tiles(prob[first + k, c, :].astype(jnp.float32)) for k in range(n)], [])
            tiles = [x * (y - delta) for x, y in zip(p, d_prob)]
            per = len(tiles) // n
            for k in range(n):
                block = jnp.concatenate(tiles[k * per : (k + 1) * per], axis=1)
                ds_rows[first + k, c, :] = block.astype(jnp.bfloat16)
        for k in range(n):
            b = first + k
            pltpu.make_async_copy(ds_rows.at[b], ds_out.at[b], sems.at[b]).start()
            slot = order[first + k]
            d_keys = jnp.transpose(dot(q_cols[...], ds_rows[first + k]) * LN2)
            d_keys = d_keys.astype(jnp.bfloat16)
            d_values = jnp.transpose(dot(g_cols[...], prob[first + k])).astype(jnp.bfloat16)
            dkv_keep[slot, :, :dim] = d_keys[:tok]
            dkv_keep[slot, :, dim:] = d_values[:tok]
            dkv_give[slot, :, :dim] = d_keys[tok:]
            dkv_give[slot, :, dim:] = d_values[tok:]

    by_pairs(count, grads_of)

    @pl.loop(0, count)
    def _(b):
        pltpu.make_async_copy(ds_rows.at[b], ds_out.at[b], sems.at[b]).wait()


def finish(
    plan, ds_in, kv_mine, kv_mate, dq_keep, dq_give, order, ds_rows, acc, sems,
    *, tok, heads, dim, group,
):
    count, _ = visible_slots(plan, order, order.shape[0])

    @pl.loop(0, count)
    def _(b):
        pltpu.make_async_copy(ds_in.at[b], ds_rows.at[b], sems.at[b]).start()

    half = heads * tok
    chunks = [slice(r, r + group) for r in range(0, 2 * half, group)]
    acc[...] = jnp.zeros_like(acc)

    def add(first, n):
        keys = stacked(order, first, n, slice(0, dim), kv_mine, kv_mate)
        for k in range(n):
            b = first + k
            pltpu.make_async_copy(ds_in.at[b], ds_rows.at[b], sems.at[b]).wait()
        for c in chunks:
            ds = jnp.concatenate([ds_rows[first + k, c, :] for k in range(n)], axis=1)
            acc[c, :] += dot(ds, keys)

    by_pairs(count, add)
    for j in range(2 * heads):
        h = slice((j % heads) * dim, (j % heads + 1) * dim)
        dq = dq_keep if j < heads else dq_give
        dq[:, h] = (acc[j * tok : (j + 1) * tok, :] / math.sqrt(dim)).astype(jnp.bfloat16)


def spread(keys, values, out):
    both = jnp.concatenate([keys[...], values[...]], axis=1)
    for n in range(out.shape[0]):
        out[n] = both


SMEM_SPEC = pl.BlockSpec(memory_space=pltpu.SMEM)
HBM_SPEC = pl.BlockSpec(memory_space=pltpu.HBM)
VMEM_SPEC = pl.BlockSpec(memory_space=pltpu.VMEM)


def sizes_of(q_raw, kv_mine):
    n_rows, dim = q_raw.shape
    spans, tok, _ = kv_mine.shape
    return spans, tok, dim, n_rows // (2 * tok), n_rows


def small_params(limit=SMALL_LIMIT):
    return pltpu.CompilerParams(vmem_limit_bytes=limit)


def row_squares_call(queries, q_mate):
    return pl.pallas_call(
        row_squares,
        out_shape=jax.ShapeDtypeStruct((2, queries.shape[0]), jnp.float32),
        in_specs=[VMEM_SPEC] * 2,
        out_specs=VMEM_SPEC,
        compiler_params=small_params(),
        cost_estimate=LONG,
        name="row_squares",
    )(queries, q_mate)


def prepare_call(queries, q_mate, out_grad, g_mate, dim):
    tok, local = queries.shape
    heads = local // dim
    rows = jax.ShapeDtypeStruct((2 * heads * tok, dim), jnp.bfloat16)
    return pl.pallas_call(
        functools.partial(prepare, tok=tok, heads=heads, dim=dim),
        out_shape=(rows, rows),
        in_specs=[VMEM_SPEC] * 4,
        out_specs=(VMEM_SPEC,) * 2,
        compiler_params=small_params(),
        cost_estimate=SHORT,
        name="prepare",
    )(queries, q_mate, out_grad, g_mate)


def merge_call(*parts):
    rows = jax.ShapeDtypeStruct(parts[0].shape, jnp.bfloat16)
    return pl.pallas_call(
        merge,
        out_shape=(rows, rows),
        in_specs=[VMEM_SPEC] * 4,
        out_specs=(VMEM_SPEC,) * 2,
        compiler_params=small_params(),
        cost_estimate=SHORT,
        name="merge",
    )(*parts)


def forward_call(plan, square_sum, gain, q_raw, g_raw, kv_mine, kv_mate, width, group=384):
    spans, tok, dim, heads, n_rows = sizes_of(q_raw, kv_mine)
    stat_rows = -(-2 * heads * STATS // 16) * 16
    return pl.pallas_call(
        functools.partial(forward, tok=tok, heads=heads, dim=dim, group=group, width=width),
        out_shape=(
            jax.ShapeDtypeStruct((spans, n_rows, 2 * tok), jnp.bfloat16),
            jax.ShapeDtypeStruct((n_rows, dim), jnp.float32),
            jax.ShapeDtypeStruct((stat_rows, LANES), jnp.float32),
            jax.ShapeDtypeStruct((n_rows, dim), jnp.bfloat16),
        ),
        in_specs=[SMEM_SPEC] + [VMEM_SPEC] * 6,
        out_specs=(HBM_SPEC, VMEM_SPEC, VMEM_SPEC, VMEM_SPEC),
        scratch_shapes=[
            pltpu.SMEM((spans,), jnp.int32),
            pltpu.VMEM((spans, n_rows, 2 * tok), jnp.float32),
            pltpu.VMEM((spans, n_rows, 2 * tok), jnp.bfloat16),
            pltpu.VMEM((n_rows, LANES), jnp.float32),
            pltpu.VMEM((n_rows, LANES), jnp.float32),
            pltpu.SemaphoreType.DMA((spans,)),
        ],
        compiler_params=pltpu.CompilerParams(vmem_limit_bytes=VMEM_LIMIT),
        name="attend_forward",
    )(plan, square_sum, gain, q_raw, g_raw, kv_mine, kv_mate)


def backward_call(
    plan, prob, stats_own, stats_mate, acc, q_rows, g_raw, kv_mine, kv_mate, group=768
):
    spans, tok, dim, heads, n_rows = sizes_of(q_rows, kv_mine)
    rows = jax.ShapeDtypeStruct((tok, heads * dim), jnp.bfloat16)
    part = jax.ShapeDtypeStruct(kv_mine.shape, jnp.bfloat16)
    return pl.pallas_call(
        functools.partial(backward, tok=tok, heads=heads, dim=dim, group=group),
        out_shape=(rows, rows, jax.ShapeDtypeStruct(prob.shape, jnp.bfloat16), part, part),
        in_specs=[SMEM_SPEC, HBM_SPEC] + [VMEM_SPEC] * 7,
        out_specs=(VMEM_SPEC, VMEM_SPEC, HBM_SPEC, VMEM_SPEC, VMEM_SPEC),
        scratch_shapes=[
            pltpu.SMEM((spans,), jnp.int32),
            pltpu.VMEM((n_rows, dim), jnp.bfloat16),
            pltpu.VMEM(prob.shape, jnp.bfloat16),
            pltpu.VMEM(prob.shape, jnp.bfloat16),
            pltpu.VMEM((n_rows, LANES), jnp.float32),
            pltpu.VMEM((dim, n_rows), jnp.bfloat16),
            pltpu.VMEM((dim, n_rows), jnp.bfloat16),
            pltpu.SemaphoreType.DMA((spans,)),
            pltpu.SemaphoreType.DMA((spans,)),
        ],
        compiler_params=small_params(VMEM_LIMIT),
        name="attend_backward",
    )(plan, prob, stats_own, stats_mate, acc, q_rows, g_raw, kv_mine, kv_mate)


def finish_call(plan, ds_rows, kv_mine, kv_mate, group=768):
    spans, n_rows, _ = ds_rows.shape
    _, tok, both = kv_mine.shape
    dim = both // 2
    heads = n_rows // (2 * tok)
    rows = jax.ShapeDtypeStruct((tok, heads * dim), jnp.bfloat16)
    return pl.pallas_call(
        functools.partial(finish, tok=tok, heads=heads, dim=dim, group=group),
        out_shape=(rows, rows),
        in_specs=[SMEM_SPEC, HBM_SPEC, VMEM_SPEC, VMEM_SPEC],
        out_specs=(VMEM_SPEC,) * 2,
        scratch_shapes=[
            pltpu.SMEM((spans,), jnp.int32),
            pltpu.VMEM(ds_rows.shape, jnp.bfloat16),
            pltpu.VMEM((n_rows, dim), jnp.float32),
            pltpu.SemaphoreType.DMA((spans,)),
        ],
        compiler_params=small_params(VMEM_LIMIT),
        cost_estimate=LONG,
        name="attend_finish",
    )(plan, ds_rows, kv_mine, kv_mate)


def spread_call(keys, values, n_z):
    tok, dim = keys.shape
    return pl.pallas_call(
        spread,
        out_shape=jax.ShapeDtypeStruct((n_z, tok, 2 * dim), jnp.bfloat16),
        in_specs=[VMEM_SPEC] * 2,
        out_specs=VMEM_SPEC,
        name="spread",
    )(keys, values)


def head_sum(x):
    x = x + lax.ppermute(x, "xl", SWAP)
    n = lax.axis_size("y")
    others = [lax.ppermute(x, "y", [(i, (i + d) % n) for i in range(n)]) for d in range(1, n)]
    return functools.reduce(jnp.add, others, x)


def shards(
    queries, key_states, value_states, out_grad, norm_gain, mask_kind, range_start, placement
):
    tok, local = queries.shape
    dim = key_states.shape[1]
    n_heads = lax.axis_size(HEAD)
    n_z = lax.axis_size("z")
    places = [lax.axis_index(a).astype(jnp.int32)[None] for a in CTX]
    plan = jnp.concatenate(places + [mask_kind, range_start, placement])

    q_mate = lax.ppermute(queries, "xh", SWAP)
    g_mate = lax.ppermute(out_grad, "xh", SWAP)
    kv_mine = lax.all_to_all(spread_call(key_states, value_states, n_z), "z", 0, 0)
    square_sum = head_sum(row_squares_call(queries, q_mate))
    q_raw, g_raw = prepare_call(queries, q_mate, out_grad, g_mate, dim)
    kv_mine, square_sum, q_raw, g_raw = lax.optimization_barrier(
        (kv_mine, square_sum, q_raw, g_raw)
    )
    kv_mate = lax.ppermute(kv_mine, "core", SWAP)

    prob, acc, stats, q_rows = forward_call(
        plan, square_sum, norm_gain[None, :], q_raw, g_raw, kv_mine, kv_mate, local * n_heads
    )
    stats_mate = lax.ppermute(stats, "xh", SWAP)
    out_keep, out_give, ds_rows, dkv_keep, dkv_give = backward_call(
        plan, prob, stats, stats_mate, acc, q_rows, g_raw, kv_mine, kv_mate
    )
    out_got = lax.ppermute(out_give, "xh", SWAP)
    dkv_got = lax.ppermute(dkv_give, "core", SWAP)
    chip = (dkv_keep.astype(jnp.float32) + dkv_got.astype(jnp.float32)).astype(jnp.bfloat16)
    chip, ds_rows = lax.optimization_barrier((chip, ds_rows))
    pieces = lax.all_to_all(chip, "z", 0, 0)
    dq_keep, dq_give = finish_call(plan, ds_rows, kv_mine, kv_mate)
    dq_got = lax.ppermute(dq_give, "xh", SWAP)
    attn_out, d_queries = merge_call(out_keep, out_got, dq_keep, dq_got)
    total = jnp.sum(pieces.astype(jnp.float32), axis=0).astype(jnp.bfloat16)
    return (attn_out, d_queries, total[:, :dim], total[:, dim:])


def solution(mesh):
    fine = Mesh(mesh.devices.reshape(8, 2, 2, 4, 2), ("z", "xh", "core", "y", "xl"))
    rows = P(CTX, HEAD)
    in_specs = (rows, rows, rows, rows, P(HEAD), P(), P(), P())
    out_specs = (rows, rows, rows, rows)
    return jax.shard_map(shards, mesh=fine, in_specs=in_specs, out_specs=out_specs, check_vma=False)
```

profile of v0, /device:TPU:1, one launch (start us, length us, event | category | flops | bytes accessed | tf_op | source)
XLA Modules:
  0.0 78.5 jit_solution(4810197413379384260)
XLA Ops:
  0.6 3.7 %collective-permute-start = (bf16[128,768]{1,0:T(8,128)(2,1)}, bf16[128,768]{1,0:T(8,128)(2,1)S(1)}, u32[]{:S(2)}, u32[]{:S(2)}) collective-permute-start(bf16[128,768]{1,0:T(8,128)(2,1)} %queries.3), channel_id=1, source_target_pairs={{0,16},{16,0},{1,17},{17,1},{2,18},{18,2},{3,19},{19,3},{4,20},{20... | collective-permute-start | bytes 589832 | tf_op jit(solution)/shard_map/ppermute | solution.py:482
  4.3 0.1 collective-permute-start.5
  4.4 1.6 %spread.1 = bf16[8,128,256]{2,1,0:T(8,128)(2,1)} custom-call(bf16[128,128]{1,0:T(8,128)(2,1)} %keys.1, bf16[128,128]{1,0:T(8,128)(2,1)} %values.1), custom_call_target="tpu_custom_call" | custom-call | tf_op jit(solution)/shard_map/spread/pallas_call | solution.py:456
  6.0 8.3 %all-to-all-start = ((bf16[8,128,256]{2,1,0:T(8,128)(2,1)}), bf16[8,128,256]{2,1,0:T(8,128)(2,1)S(1)}, u32[]{:S(2)}, u32[]{:S(2)}) async-start(bf16[8,128,256]{2,1,0:T(8,128)(2,1)} %spread.1), calls=%async_computation | async-start | bytes 1048576 | tf_op jit(solution)/shard_map/all_to_all | solution.py:484
  14.3 0.9 %copy-done = bf16[128,768]{1,0:T(8,128)(2,1)S(1)} copy-done((bf16[128,768]{1,0:T(8,128)(2,1)S(1)}, bf16[128,768]{1,0:T(8,128)(2,1)}, u32[]{:S(2)}) %copy-start) | copy-done | bytes 196632
  15.3 0.2 row_squares.1
  15.4 1.3 %collective-permute-start.1 = (f32[2,128]{1,0:T(2,128)S(1)}, f32[2,128]{1,0:T(2,128)S(1)}, u32[]{:S(2)}, u32[]{:S(2)}) collective-permute-start(f32[2,128]{1,0:T(2,128)S(1)} %row_squares.1), channel_id=1, source_target_pairs={{0,1},{1,0},{2,3},{3,2},{4,5},{5,4},{6,7},{7,6},{8,9},{9,8},{10,11... | collective-permute-start | bytes 3080 | tf_op jit(solution)/shard_map/ppermute | solution.py:466
  16.7 1.2 %collective-permute-done.1 = f32[2,128]{1,0:T(2,128)S(1)} collective-permute-done((f32[2,128]{1,0:T(2,128)S(1)}, f32[2,128]{1,0:T(2,128)S(1)}, u32[]{:S(2)}, u32[]{:S(2)}) %collective-permute-start.1) | collective-permute-done | bytes 1056 | tf_op jit(solution)/shard_map/ppermute | solution.py:466
  17.9 2.7 %collective-permute-start.4 = (f32[2,128]{1,0:T(2,128)S(1)}, f32[2,128]{1,0:T(2,128)S(1)}, u32[]{:S(2)}, u32[]{:S(2)}) collective-permute-start(f32[2,128]{1,0:T(2,128)S(1)} %add.15), channel_id=1, source_target_pairs={{0,6},{2,0},{4,2},{6,4},{1,7},{3,1},{5,3},{7,5},{8,14},{10,8},{12,... | collective-permute-start | bytes 3080 | tf_op jit(solution)/shard_map/ppermute | solution.py:468
  20.7 0.3 collective-permute-start.3
  21.0 0.7 collective-permute-start.2
  21.7 0.1 prepare.1
  21.9 3.0 %collective-permute-done.3 = f32[2,128]{1,0:T(2,128)S(1)} collective-permute-done((f32[2,128]{1,0:T(2,128)S(1)}, f32[2,128]{1,0:T(2,128)S(1)}, u32[]{:S(2)}, u32[]{:S(2)}) %collective-permute-start.3) | collective-permute-done | bytes 1056 | tf_op jit(solution)/shard_map/ppermute | solution.py:468
  25.0 5.8 %all-to-all-done.kv_mine = bf16[8,128,256]{2,1,0:T(8,128)(2,1)S(1)} async-done(((bf16[8,128,256]{2,1,0:T(8,128)(2,1)}), bf16[8,128,256]{2,1,0:T(8,128)(2,1)S(1)}, u32[]{:S(2)}, u32[]{:S(2)}) %all-to-all-start) | async-done | bytes 524320 | tf_op jit(solution)/shard_map/all_to_all | solution.py:484
  30.7 2.0 %collective-permute-start.6 = (bf16[8,128,256]{2,1,0:T(8,128)(2,1)S(1)}, bf16[8,128,256]{2,1,0:T(8,128)(2,1)S(1)}, u32[]{:S(2)}, u32[]{:S(2)}) collective-permute-start(bf16[8,128,256]{2,1,0:T(8,128)(2,1)S(1)} %all-to-all-done.kv_mine), channel_id=1, source_target_pairs={{0,8},{8,0},{1,9},{9,1},{2,10},{10,2},{3,11},{11,3},{4,12},{12,4},... | collective-permute-start | bytes 1572872 | tf_op jit(solution)/shard_map/ppermute | solution.py:490
  32.8 0.1 concatenate.3.plan
  32.9 1.4 %collective-permute-done.6.kv_mate = bf16[8,128,256]{2,1,0:T(8,128)(2,1)S(1)} collective-permute-done((bf16[8,128,256]{2,1,0:T(8,128)(2,1)S(1)}, bf16[8,128,256]{2,1,0:T(8,128)(2,1)S(1)}, u32[]{:S(2)}, u32[]{:S(2)}) %collective-permute-start.6) | collective-permute-done | bytes 524320 | tf_op jit(solution)/shard_map/ppermute | solution.py:490
  34.3 6.1 %attend_forward.1 = (bf16[8,1536,256]{2,1,0:T(8,128)(2,1)}, f32[1536,128]{1,0:T(8,128)S(1)}, f32[48,128]{1,0:T(8,128)S(1)}, bf16[1536,128]{1,0:T(8,128)(2,1)S(1)}) custom-call(s32[27]{0:T(128)S(1)} %concatenate.3.plan, f32[2,128]{1,0:T(2,128)S(1)} %add_add_fusion.square_sum, f32[1,768]{1,0:T(1,128)S(1)} %broadcast_in_dim.15.gain, ...), custom_call_target="tpu_custom_call" | custom-call | tf_op jit(solution)/shard_map/attend_forward/pallas_call | solution.py:381
  40.4 2.8 %collective-permute-start.7 = (f32[48,128]{1,0:T(8,128)S(1)}, f32[48,128]{1,0:T(8,128)S(1)}, u32[]{:S(2)}, u32[]{:S(2)}) collective-permute-start(f32[48,128]{1,0:T(8,128)S(1)} %get-tuple-element.32.stats_own), channel_id=1, source_target_pairs={{0,16},{16,0},{1,17},{17,1},{2,18},{18,2},{3,19},{19,3},{4,20},{20... | collective-permute-start | bytes 73736 | tf_op jit(solution)/shard_map/ppermute | solution.py:495
  43.2 1.4 %collective-permute-done.7.stats_mate = f32[48,128]{1,0:T(8,128)S(1)} collective-permute-done((f32[48,128]{1,0:T(8,128)S(1)}, f32[48,128]{1,0:T(8,128)S(1)}, u32[]{:S(2)}, u32[]{:S(2)}) %collective-permute-start.7) | collective-permute-done | bytes 24608 | tf_op jit(solution)/shard_map/ppermute | solution.py:495
  44.7 6.4 %attend_backward.1 = (bf16[128,768]{1,0:T(8,128)(2,1)S(1)}, bf16[128,768]{1,0:T(8,128)(2,1)S(1)}, bf16[8,1536,256]{2,1,0:T(8,128)(2,1)}, bf16[8,128,256]{2,1,0:T(8,128)(2,1)S(1)}, bf16[8,128,256]{2,1,0:T(8,128)(2,1)S(1)}) custom-call(s32[27]{0:T(128)S(1)} %concatenate.3.plan, bf16[8,1536,256]{2,1,0:T(8,128)(2,1)} %get-tuple-element.31.prob_in, ...), custom_call_target="tpu_custom_call" | custom-call | tf_op jit(solution)/shard_map/attend_backward/pallas_call | solution.py:410
  51.1 1.6 %collective-permute-start.9 = (bf16[8,128,256]{2,1,0:T(8,128)(2,1)S(1)}, bf16[8,128,256]{2,1,0:T(8,128)(2,1)S(1)}, u32[]{:S(2)}, u32[]{:S(2)}) collective-permute-start(bf16[8,128,256]{2,1,0:T(8,128)(2,1)S(1)} %get-tuple-element.38), channel_id=1, source_target_pairs={{0,8},{8,0},{1,9},{9,1},{2,10},{10,2},{3,11},{11,3},{4,12},{12,4},... | collective-permute-start | bytes 1572872 | tf_op jit(solution)/shard_map/ppermute | solution.py:500
  52.7 2.8 %collective-permute-start.8 = (bf16[128,768]{1,0:T(8,128)(2,1)S(1)}, bf16[128,768]{1,0:T(8,128)(2,1)S(1)}, u32[]{:S(2)}, u32[]{:S(2)}) collective-permute-start(bf16[128,768]{1,0:T(8,128)(2,1)S(1)} %get-tuple-element.36), channel_id=1, source_target_pairs={{0,16},{16,0},{1,17},{17,1},{2,18},{18,2},{3,19},{19,3},{4,20},{20... | collective-permute-start | bytes 589832 | tf_op jit(solution)/shard_map/ppermute | solution.py:499
  55.5 1.0 %add_convert_fusion = bf16[8,128,256]{2,1,0:T(8,128)(2,1)} fusion(bf16[8,128,256]{2,1,0:T(8,128)(2,1)S(1)} %collective-permute-done.9, bf16[8,128,256]{2,1,0:T(8,128)(2,1)S(1)} %get-tuple-element.37), kind=kLoop, calls=%fused_computation | loop fusion | flops 1048576 | bytes 1572864 | tf_op jit(solution)/shard_map/convert_element_type | solution.py:501
  56.4 3.5 %all-to-all-start.1 = ((bf16[8,128,256]{2,1,0:T(8,128)(2,1)}), bf16[8,128,256]{2,1,0:T(8,128)(2,1)S(1)}, u32[]{:S(2)}, u32[]{:S(2)}) async-start(bf16[8,128,256]{2,1,0:T(8,128)(2,1)} %add_convert_fusion), calls=%async_computation.1 | async-start | bytes 1048576 | tf_op jit(solution)/shard_map/all_to_all | solution.py:503
  59.9 3.9 %attend_finish.1 = (bf16[128,768]{1,0:T(8,128)(2,1)S(1)}, bf16[128,768]{1,0:T(8,128)(2,1)S(1)}) custom-call(s32[27]{0:T(128)S(1)} %concatenate.3.plan, bf16[8,1536,256]{2,1,0:T(8,128)(2,1)} %get-tuple-element.40.ds_in, bf16[8,128,256]{2,1,0:T(8,128)(2,1)S(1)} %all-to-all-done.kv_mine, bf16[8,128,256]{2,1,0:T(8,128)(2,1)S(1)} %collective-permute-done.6.kv_mate), custom_call_target="tpu_custom_call" | custom-call | flops 20000000000 | bytes 1048576 | tf_op jit(solution)/shard_map/attend_finish/pallas_call | solution.py:437
  63.8 1.6 %collective-permute-start.10 = (bf16[128,768]{1,0:T(8,128)(2,1)S(1)}, bf16[128,768]{1,0:T(8,128)(2,1)S(1)}, u32[]{:S(2)}, u32[]{:S(2)}) collective-permute-start(bf16[128,768]{1,0:T(8,128)(2,1)S(1)} %get-tuple-element.42), channel_id=1, source_target_pairs={{0,16},{16,0},{1,17},{17,1},{2,18},{18,2},{3,19},{19,3},{4,20},{20... | collective-permute-start | bytes 589832 | tf_op jit(solution)/shard_map/ppermute | solution.py:505
  65.4 5.9 %collective-permute-done.10.dq_got = bf16[128,768]{1,0:T(8,128)(2,1)S(1)} collective-permute-done((bf16[128,768]{1,0:T(8,128)(2,1)S(1)}, bf16[128,768]{1,0:T(8,128)(2,1)S(1)}, u32[]{:S(2)}, u32[]{:S(2)}) %collective-permute-start.10) | collective-permute-done | bytes 196640 | tf_op jit(solution)/shard_map/ppermute | solution.py:505
  71.3 0.8 %merge.1 = (bf16[128,768]{1,0:T(8,128)(2,1)}, bf16[128,768]{1,0:T(8,128)(2,1)}) custom-call(bf16[128,768]{1,0:T(8,128)(2,1)S(1)} %get-tuple-element.35.out_keep, bf16[128,768]{1,0:T(8,128)(2,1)S(1)} %collective-permute-done.8.out_got, bf16[128,768]{1,0:T(8,128)(2,1)S(1)} %get-tuple-element.41.dq_keep, bf16[128,768]{1,0:T(8,128)(2,1)S(1)} %collective-permute-done.10.dq_got), custom_call_target="tpu_custom_call" | custom-call | flops 1024 | bytes 1024 | tf_op jit(solution)/shard_map/merge/pallas_call | solution.py:367
  72.1 5.7 %all-to-all-done.1 = bf16[8,128,256]{2,1,0:T(8,128)(2,1)S(1)} async-done(((bf16[8,128,256]{2,1,0:T(8,128)(2,1)}), bf16[8,128,256]{2,1,0:T(8,128)(2,1)S(1)}, u32[]{:S(2)}, u32[]{:S(2)}) %all-to-all-start.1) | async-done | bytes 524320 | tf_op jit(solution)/shard_map/all_to_all | solution.py:503
  77.8 0.1 reduce_sum.12
  77.9 0.6 fusion
  (22 shorter events, 0.1 us)
Async XLA Ops:
  0.6 13.7 %collective-permute-start = (bf16[128,768]{1,0:T(8,128)(2,1)}, bf16[128,768]{1,0:T(8,128)(2,1)S(1)}, u32[]{:S(2)}, u32[]{:S(2)}) collective-permute-start(bf16[128,768]{1,0:T(8,128)(2,1)} %queries.3), channel_id=1, source_target_pairs={{0,16},{16,0},{1,17},{17,1},{2,18},{18,2},{3,19},{19,3},{4,20},{20... | collective-permute-start | bytes 589832 | tf_op jit(solution)/shard_map/ppermute | solution.py:482
  4.3 17.4 %collective-permute-start.5 = (bf16[128,768]{1,0:T(8,128)(2,1)}, bf16[128,768]{1,0:T(8,128)(2,1)S(1)}, u32[]{:S(2)}, u32[]{:S(2)}) collective-permute-start(bf16[128,768]{1,0:T(8,128)(2,1)} %out_grad.1), channel_id=1, source_target_pairs={{0,16},{16,0},{1,17},{17,1},{2,18},{18,2},{3,19},{19,3},{4,20},{20... | collective-permute-start | bytes 589832 | tf_op jit(solution)/shard_map/ppermute | solution.py:483
  6.0 24.7 %all-to-all-start = ((bf16[8,128,256]{2,1,0:T(8,128)(2,1)}), bf16[8,128,256]{2,1,0:T(8,128)(2,1)S(1)}, u32[]{:S(2)}, u32[]{:S(2)}) async-start(bf16[8,128,256]{2,1,0:T(8,128)(2,1)} %spread.1), calls=%async_computation | async-start | bytes 1048576 | tf_op jit(solution)/shard_map/all_to_all | solution.py:484
  14.3 0.9 %copy-start = (bf16[128,768]{1,0:T(8,128)(2,1)S(1)}, bf16[128,768]{1,0:T(8,128)(2,1)}, u32[]{:S(2)}) copy-start(bf16[128,768]{1,0:T(8,128)(2,1)} %queries.3) | copy-start | bytes 589828
  15.3 6.5 %copy-start.1 = (bf16[128,768]{1,0:T(8,128)(2,1)S(1)}, bf16[128,768]{1,0:T(8,128)(2,1)}, u32[]{:S(2)}) copy-start(bf16[128,768]{1,0:T(8,128)(2,1)} %queries.3) | copy-start | bytes 589828
  15.3 6.5 %copy-start.2 = (bf16[128,768]{1,0:T(8,128)(2,1)S(1)}, bf16[128,768]{1,0:T(8,128)(2,1)}, u32[]{:S(2)}) copy-start(bf16[128,768]{1,0:T(8,128)(2,1)} %out_grad.1) | copy-start | bytes 589828
  15.3 17.5 %copy-start.3 = (f32[768]{0:T(1024)S(1)}, f32[768]{0:T(1024)}, u32[]{:S(2)}) copy-start(f32[768]{0:T(1024)} %param.12) | copy-start | bytes 9220
  15.3 17.5 %copy-start.4 = (s32[8]{0:T(128)S(1)}, s32[8]{0:T(128)}, u32[]{:S(2)}) copy-start(s32[8]{0:T(128)} %param.13) | copy-start | bytes 100
  15.3 17.5 %copy-start.5 = (s32[8]{0:T(128)S(1)}, s32[8]{0:T(128)}, u32[]{:S(2)}) copy-start(s32[8]{0:T(128)} %param.14) | copy-start | bytes 100
  15.3 17.5 %copy-start.6 = (s32[8]{0:T(128)S(1)}, s32[8]{0:T(128)}, u32[]{:S(2)}) copy-start(s32[8]{0:T(128)} %param.15) | copy-start | bytes 100
  15.4 2.5 %collective-permute-start.1 = (f32[2,128]{1,0:T(2,128)S(1)}, f32[2,128]{1,0:T(2,128)S(1)}, u32[]{:S(2)}, u32[]{:S(2)}) collective-permute-start(f32[2,128]{1,0:T(2,128)S(1)} %row_squares.1), channel_id=1, source_target_pairs={{0,1},{1,0},{2,3},{3,2},{4,5},{5,4},{6,7},{7,6},{8,9},{9,8},{10,11... | collective-permute-start | bytes 3080 | tf_op jit(solution)/shard_map/ppermute | solution.py:466
  17.9 3.9 %collective-permute-start.4 = (f32[2,128]{1,0:T(2,128)S(1)}, f32[2,128]{1,0:T(2,128)S(1)}, u32[]{:S(2)}, u32[]{:S(2)}) collective-permute-start(f32[2,128]{1,0:T(2,128)S(1)} %add.15), channel_id=1, source_target_pairs={{0,6},{2,0},{4,2},{6,4},{1,7},{3,1},{5,3},{7,5},{8,14},{10,8},{12,... | collective-permute-start | bytes 3080 | tf_op jit(solution)/shard_map/ppermute | solution.py:468
  20.7 4.2 %collective-permute-start.3 = (f32[2,128]{1,0:T(2,128)S(1)}, f32[2,128]{1,0:T(2,128)S(1)}, u32[]{:S(2)}, u32[]{:S(2)}) collective-permute-start(f32[2,128]{1,0:T(2,128)S(1)} %add.15), channel_id=1, source_target_pairs={{0,4},{2,6},{4,0},{6,2},{1,5},{3,7},{5,1},{7,3},{8,12},{10,14},{12... | collective-permute-start | bytes 3080 | tf_op jit(solution)/shard_map/ppermute | solution.py:468
  21.0 3.9 %collective-permute-start.2 = (f32[2,128]{1,0:T(2,128)S(1)}, f32[2,128]{1,0:T(2,128)S(1)}, u32[]{:S(2)}, u32[]{:S(2)}) collective-permute-start(f32[2,128]{1,0:T(2,128)S(1)} %add.15), channel_id=1, source_target_pairs={{0,2},{2,4},{4,6},{6,0},{1,3},{3,5},{5,7},{7,1},{8,10},{10,12},{12... | collective-permute-start | bytes 3080 | tf_op jit(solution)/shard_map/ppermute | solution.py:468
  30.7 3.6 %collective-permute-start.6 = (bf16[8,128,256]{2,1,0:T(8,128)(2,1)S(1)}, bf16[8,128,256]{2,1,0:T(8,128)(2,1)S(1)}, u32[]{:S(2)}, u32[]{:S(2)}) collective-permute-start(bf16[8,128,256]{2,1,0:T(8,128)(2,1)S(1)} %all-to-all-done.kv_mine), channel_id=1, source_target_pairs={{0,8},{8,0},{1,9},{9,1},{2,10},{10,2},{3,11},{11,3},{4,12},{12,4},... | collective-permute-start | bytes 1572872 | tf_op jit(solution)/shard_map/ppermute | solution.py:490
  40.4 4.3 %collective-permute-start.7 = (f32[48,128]{1,0:T(8,128)S(1)}, f32[48,128]{1,0:T(8,128)S(1)}, u32[]{:S(2)}, u32[]{:S(2)}) collective-permute-start(f32[48,128]{1,0:T(8,128)S(1)} %get-tuple-element.32.stats_own), channel_id=1, source_target_pairs={{0,16},{16,0},{1,17},{17,1},{2,18},{18,2},{3,19},{19,3},{4,20},{20... | collective-permute-start | bytes 73736 | tf_op jit(solution)/shard_map/ppermute | solution.py:495
  51.1 4.4 %collective-permute-start.9 = (bf16[8,128,256]{2,1,0:T(8,128)(2,1)S(1)}, bf16[8,128,256]{2,1,0:T(8,128)(2,1)S(1)}, u32[]{:S(2)}, u32[]{:S(2)}) collective-permute-start(bf16[8,128,256]{2,1,0:T(8,128)(2,1)S(1)} %get-tuple-element.38), channel_id=1, source_target_pairs={{0,8},{8,0},{1,9},{9,1},{2,10},{10,2},{3,11},{11,3},{4,12},{12,4},... | collective-permute-start | bytes 1572872 | tf_op jit(solution)/shard_map/ppermute | solution.py:500
  52.7 12.8 %collective-permute-start.8 = (bf16[128,768]{1,0:T(8,128)(2,1)S(1)}, bf16[128,768]{1,0:T(8,128)(2,1)S(1)}, u32[]{:S(2)}, u32[]{:S(2)}) collective-permute-start(bf16[128,768]{1,0:T(8,128)(2,1)S(1)} %get-tuple-element.36), channel_id=1, source_target_pairs={{0,16},{16,0},{1,17},{17,1},{2,18},{18,2},{3,19},{19,3},{4,20},{20... | collective-permute-start | bytes 589832 | tf_op jit(solution)/shard_map/ppermute | solution.py:499
  56.4 21.4 %all-to-all-start.1 = ((bf16[8,128,256]{2,1,0:T(8,128)(2,1)}), bf16[8,128,256]{2,1,0:T(8,128)(2,1)S(1)}, u32[]{:S(2)}, u32[]{:S(2)}) async-start(bf16[8,128,256]{2,1,0:T(8,128)(2,1)} %add_convert_fusion), calls=%async_computation.1 | async-start | bytes 1048576 | tf_op jit(solution)/shard_map/all_to_all | solution.py:503
  63.8 7.5 %collective-permute-start.10 = (bf16[128,768]{1,0:T(8,128)(2,1)S(1)}, bf16[128,768]{1,0:T(8,128)(2,1)S(1)}, u32[]{:S(2)}, u32[]{:S(2)}) collective-permute-start(bf16[128,768]{1,0:T(8,128)(2,1)S(1)} %get-tuple-element.42), channel_id=1, source_target_pairs={{0,16},{16,0},{1,17},{17,1},{2,18},{18,2},{3,19},{19,3},{4,20},{20... | collective-permute-start | bytes 589832 | tf_op jit(solution)/shard_map/ppermute | solution.py:505
where the time goes:
time: 78.3 us; the launch traced here: 78.5 us
  starting transfers between devices  31.5 us (40%)
  waiting for transfers between devices  24.5 us (31%)
  Pallas kernels  19.1 us (24%)
  local copies, waits for them, and re-layouts  1.66 us (2%)
  other arithmetic  1.03 us (1%)
    all_to_all x1, starting transfers between devices, shards(): lax.all_to_all(spread_call(key_states, value_states, n_z), 'z', 0, 0)  8.31 us
    pallas_call x1, Pallas kernels, backward_call(): pl.pallas_call(functools.partial(backward, tok=tok, heads=heads, dim=dim,...  6.41 us
    pallas_call x1, Pallas kernels, forward_call(): pl.pallas_call(functools.partial(forward, tok=tok, heads=heads, dim=dim,...  6.08 us
    ppermute x1, waiting for transfers between devices, shards(): dq_got = lax.ppermute(dq_give, 'xh', SWAP)  5.85 us
    all_to_all x1, waiting for transfers between devices, shards(): lax.all_to_all(spread_call(key_states, value_states, n_z), 'z', 0, 0)  5.76 us
    all_to_all x1, waiting for transfers between devices, shards(): pieces = lax.all_to_all(chip, 'z', 0, 0)  5.71 us
    pallas_call x1, Pallas kernels, finish_call(): pl.pallas_call(functools.partial(finish, tok=tok, heads=heads, dim=dim, g...  3.93 us
    ppermute x3, starting transfers between devices, head_sum(): lax.ppermute(x, 'y', [(i, (i + d) % n) for i in range(n)])  3.77 us
  transfers between devices with their start and end apart: 13, of which 8 were waited for; matrix products, arithmetic and copies ran while one was open for 1% of the time, Pallas kernels for 8%

commit v1 on v0

--- a/solution.py
+++ b/solution.py
@@ -19,9 +19,11 @@
 CTX = ("z", "xh", "core")
 HEAD = ("y", "xl")
 SWAP = [(0, 1), (1, 0)]
-VMEM_LIMIT = 48 * 2**20
+VMEM_LIMIT = 24 * 2**20
+BACKWARD_LIMIT = 18 * 2**20
 SMALL_LIMIT = 8 * 2**20
 LONG = pl.CostEstimate(flops=2 * 10**10, bytes_accessed=2**20, transcendentals=0)
+MEDIUM = pl.CostEstimate(flops=3 * 10**9, bytes_accessed=2**10, transcendentals=0)
 SHORT = pl.CostEstimate(flops=2**10, bytes_accessed=2**10, transcendentals=0)
 
 
@@ -94,11 +96,27 @@
     return jnp.transpose(jnp.concatenate([table, pad], axis=0))
 
 
-def row_squares(queries, q_mate, parts):
-    for side, rows_of in enumerate((queries, q_mate)):
-        wide = rows_of[...].astype(jnp.float32)
-        total = functools.reduce(jnp.add, lane_tiles(wide * wide))
-        parts[side : side + 1, :] = jnp.sum(jnp.transpose(total), axis=0, keepdims=True)
+def squares_of(rows_of):
+    wide = rows_of.astype(jnp.float32)
+    total = functools.reduce(jnp.add, lane_tiles(wide * wide))
+    return jnp.sum(jnp.transpose(total), axis=0, keepdims=True)
+
+
+def row_squares(own, q_mate, parts):
+    parts[0:1, :] = own[...]
+    parts[1:2, :] = squares_of(q_mate[...])
+
+
+def normalize(square_sum, gain, q_raw, q_rows, q_cols, *, tok, heads, dim, width):
+    sums = columns_of(square_sum[...])
+    scale = lax.rsqrt(sums / width + EPS) * (LOG2E / math.sqrt(dim))
+    for side in range(2):
+        for h in range(heads):
+            r = slice((side * heads + h) * tok, (side * heads + h + 1) * tok)
+            normed = q_raw[r, :].astype(jnp.float32) * scale[:, side : side + 1]
+            normed = (normed * gain[:, h * dim : (h + 1) * dim]).astype(jnp.bfloat16)
+            q_rows[r, :] = normed
+            q_cols[:, r] = jnp.transpose(normed)
 
 
 def prepare(queries, q_mate, out_grad, g_mate, q_raw, g_raw, *, tok, heads, dim):
@@ -115,22 +133,14 @@
 
 
 def forward(
-    plan, square_sum, gain, q_raw, g_raw, kv_mine, kv_mate,
-    prob_out, acc, stats, q_rows,
-    order, score, prob, row_max, row_sum, sems,
-    *, tok, heads, dim, group, width,
+    plan, q_rows, g_raw, kv_mine, kv_mate,
+    prob, acc, stats,
+    order, score, row_max, row_sum,
+    *, tok, heads, dim, group,
 ):
     spans = order.shape[0]
     half = heads * tok
     keys_n = 2 * tok
-    sums = columns_of(square_sum[...])
-    scale = lax.rsqrt(sums / width + EPS) * (LOG2E / math.sqrt(dim))
-    for side in range(2):
-        for h in range(heads):
-            r = slice(side * half + h * tok, side * half + (h + 1) * tok)
-            normed = q_raw[r, :].astype(jnp.float32) * scale[:, side : side + 1]
-            normed = normed * gain[:, h * dim : (h + 1) * dim]
-            q_rows[r, :] = normed.astype(jnp.bfloat16)
     count, own_span = visible_slots(plan, order, spans)
     row_max[...] = jnp.full_like(row_max, NEG)
     row_sum[...] = jnp.zeros_like(row_sum)
@@ -184,9 +194,6 @@
             for k in range(n):
                 prob[first + k, c, :] = p[k]
             acc[c, :] += dot(jnp.concatenate(p, axis=1), values)
-        for k in range(n):
-            b = first + k
-            pltpu.make_async_copy(prob.at[b], prob_out.at[b], sems.at[b]).start()
 
     by_pairs(count, weigh)
 
@@ -200,23 +207,15 @@
         table = jnp.where(lane == STATS * j + 2, lane_sum(grad * acc[r, :]), table)
     stats[...] = jnp.transpose(table)[: stats.shape[0], :]
 
-    @pl.loop(0, count)
-    def _(b):
-        pltpu.make_async_copy(prob.at[b], prob_out.at[b], sems.at[b]).wait()
-
 
 def backward(
-    plan, prob_in, stats_own, stats_mate, acc_in, q_rows, g_raw, kv_mine, kv_mate,
+    plan, prob, stats_own, stats_mate, acc_in, q_cols, g_raw, kv_mine, kv_mate,
     out_keep, out_give, ds_out, dkv_keep, dkv_give,
-    order, g_rows, prob, ds_rows, delta_rows, q_cols, g_cols, in_sems, sems,
+    order, g_rows, ds_rows, delta_rows, g_cols, sems,
     *, tok, heads, dim, group,
 ):
     spans = order.shape[0]
     count, _ = visible_slots(plan, order, spans)
-
-    @pl.loop(0, count)
-    def _(b):
-        pltpu.make_async_copy(prob_in.at[b], prob.at[b], in_sems.at[b]).start()
 
     half = heads * tok
     mine, theirs = columns_of(stats_own[...]), columns_of(stats_mate[...])
@@ -236,7 +235,6 @@
         out[:, h] = (acc_in[r, :] * scale).astype(jnp.bfloat16)
     for j in range(2 * heads):
         r = slice(j * tok, (j + 1) * tok)
-        q_cols[:, r] = jnp.transpose(q_rows[r, :])
         g_cols[:, r] = jnp.transpose(g_rows[r, :])
     chunks = [slice(r, r + group) for r in range(0, 2 * half, group)]
 
@@ -253,9 +251,6 @@
 
     def grads_of(first, n):
         values = stacked(order, first, n, slice(dim, 2 * dim), kv_mine, kv_mate)
-        for k in range(n):
-            b = first + k
-            pltpu.make_async_copy(prob_in.at[b], prob.at[b], in_sems.at[b]).wait()
         for c in chunks:
             d_prob = lane_tiles(dot_rows(g_rows[c, :], values))
             delta = delta_rows[c, :]
@@ -268,16 +263,20 @@
         for k in range(n):
             b = first + k
             pltpu.make_async_copy(ds_rows.at[b], ds_out.at[b], sems.at[b]).start()
+
+    def keys_of(first, n):
+        for k in range(n):
             slot = order[first + k]
             d_keys = jnp.transpose(dot(q_cols[...], ds_rows[first + k]) * LN2)
             d_keys = d_keys.astype(jnp.bfloat16)
+            dkv_keep[slot, :, :dim] = d_keys[:tok]
+            dkv_give[slot, :, :dim] = d_keys[tok:]
             d_values = jnp.transpose(dot(g_cols[...], prob[first + k])).astype(jnp.bfloat16)
-            dkv_keep[slot, :, :dim] = d_keys[:tok]
             dkv_keep[slot, :, dim:] = d_values[:tok]
-            dkv_give[slot, :, :dim] = d_keys[tok:]
             dkv_give[slot, :, dim:] = d_values[tok:]
 
     by_pairs(count, grads_of)
+    by_pairs(count, keys_of)
 
     @pl.loop(0, count)
     def _(b):
@@ -293,6 +292,7 @@
     @pl.loop(0, count)
     def _(b):
         pltpu.make_async_copy(ds_in.at[b], ds_rows.at[b], sems.at[b]).start()
+
 
     half = heads * tok
     chunks = [slice(r, r + group) for r in range(0, 2 * half, group)]
@@ -314,10 +314,11 @@
         dq[:, h] = (acc[j * tok : (j + 1) * tok, :] / math.sqrt(dim)).astype(jnp.bfloat16)
 
 
-def spread(keys, values, out):
+def spread(keys, values, queries, out, squares):
     both = jnp.concatenate([keys[...], values[...]], axis=1)
     for n in range(out.shape[0]):
         out[n] = both
+    squares[...] = squares_of(queries[...])
 
 
 SMEM_SPEC = pl.BlockSpec(memory_space=pltpu.SMEM)
@@ -335,16 +336,35 @@
     return pltpu.CompilerParams(vmem_limit_bytes=limit)
 
 
-def row_squares_call(queries, q_mate):
+def row_squares_call(own, q_mate):
     return pl.pallas_call(
         row_squares,
-        out_shape=jax.ShapeDtypeStruct((2, queries.shape[0]), jnp.float32),
+        out_shape=jax.ShapeDtypeStruct((2, own.shape[1]), jnp.float32),
         in_specs=[VMEM_SPEC] * 2,
         out_specs=VMEM_SPEC,
         compiler_params=small_params(),
         cost_estimate=LONG,
         name="row_squares",
-    )(queries, q_mate)
+    )(own, q_mate)
+
+
+def normalize_call(square_sum, gain, q_raw, width):
+    tok = square_sum.shape[1]
+    n_rows, dim = q_raw.shape
+    return pl.pallas_call(
+        functools.partial(
+            normalize, tok=tok, heads=n_rows // (2 * tok), dim=dim, width=width
+        ),
+        out_shape=(
+            jax.ShapeDtypeStruct((n_rows, dim), jnp.bfloat16),
+            jax.ShapeDtypeStruct((dim, n_rows), jnp.bfloat16),
+        ),
+        in_specs=[VMEM_SPEC] * 3,
+        out_specs=(VMEM_SPEC,) * 2,
+        compiler_params=small_params(),
+        cost_estimate=SHORT,
+        name="normalize",
+    )(square_sum, gain, q_raw)
 
 
 def prepare_call(queries, q_mate, out_grad, g_mate, dim):
@@ -362,6 +382,21 @@
     )(queries, q_mate, out_grad, g_mate)
 
 
+def add_pair(one, other, out):
+    out[...] = (one[...].astype(jnp.float32) + other[...].astype(jnp.float32)).astype(out.dtype)
+
+
+def add_pair_call(one, other):
+    return pl.pallas_call(
+        add_pair,
+        out_shape=jax.ShapeDtypeStruct(one.shape, jnp.bfloat16),
+        in_specs=[VMEM_SPEC] * 2,
+        out_specs=VMEM_SPEC,
+        compiler_params=small_params(),
+        name="add_pair",
+    )(one, other)
+
+
 def merge_call(*parts):
     rows = jax.ShapeDtypeStruct(parts[0].shape, jnp.bfloat16)
     return pl.pallas_call(
@@ -375,57 +410,51 @@
     )(*parts)
 
 
-def forward_call(plan, square_sum, gain, q_raw, g_raw, kv_mine, kv_mate, width, group=384):
-    spans, tok, dim, heads, n_rows = sizes_of(q_raw, kv_mine)
+def forward_call(plan, q_rows, g_raw, kv_mine, kv_mate, group=384):
+    spans, tok, dim, heads, n_rows = sizes_of(q_rows, kv_mine)
     stat_rows = -(-2 * heads * STATS // 16) * 16
     return pl.pallas_call(
-        functools.partial(forward, tok=tok, heads=heads, dim=dim, group=group, width=width),
+        functools.partial(forward, tok=tok, heads=heads, dim=dim, group=group),
         out_shape=(
             jax.ShapeDtypeStruct((spans, n_rows, 2 * tok), jnp.bfloat16),
             jax.ShapeDtypeStruct((n_rows, dim), jnp.float32),
             jax.ShapeDtypeStruct((stat_rows, LANES), jnp.float32),
-            jax.ShapeDtypeStruct((n_rows, dim), jnp.bfloat16),
         ),
-        in_specs=[SMEM_SPEC] + [VMEM_SPEC] * 6,
-        out_specs=(HBM_SPEC, VMEM_SPEC, VMEM_SPEC, VMEM_SPEC),
+        in_specs=[SMEM_SPEC] + [VMEM_SPEC] * 4,
+        out_specs=(VMEM_SPEC,) * 3,
         scratch_shapes=[
             pltpu.SMEM((spans,), jnp.int32),
             pltpu.VMEM((spans, n_rows, 2 * tok), jnp.float32),
-            pltpu.VMEM((spans, n_rows, 2 * tok), jnp.bfloat16),
             pltpu.VMEM((n_rows, LANES), jnp.float32),
             pltpu.VMEM((n_rows, LANES), jnp.float32),
-            pltpu.SemaphoreType.DMA((spans,)),
         ],
         compiler_params=pltpu.CompilerParams(vmem_limit_bytes=VMEM_LIMIT),
         name="attend_forward",
-    )(plan, square_sum, gain, q_raw, g_raw, kv_mine, kv_mate)
+    )(plan, q_rows, g_raw, kv_mine, kv_mate)
 
 
 def backward_call(
-    plan, prob, stats_own, stats_mate, acc, q_rows, g_raw, kv_mine, kv_mate, group=768
+    plan, prob, stats_own, stats_mate, acc, q_cols, g_raw, kv_mine, kv_mate, group=768
 ):
-    spans, tok, dim, heads, n_rows = sizes_of(q_rows, kv_mine)
+    spans, tok, dim, heads, n_rows = sizes_of(g_raw, kv_mine)
     rows = jax.ShapeDtypeStruct((tok, heads * dim), jnp.bfloat16)
     part = jax.ShapeDtypeStruct(kv_mine.shape, jnp.bfloat16)
     return pl.pallas_call(
         functools.partial(backward, tok=tok, heads=heads, dim=dim, group=group),
-        out_shape=(rows, rows, jax.ShapeDtypeStruct(prob.shape, jnp.bfloat16), part, part),
-        in_specs=[SMEM_SPEC, HBM_SPEC] + [VMEM_SPEC] * 7,
+        out_shape=(rows, rows, pltpu.HBM(prob.shape, jnp.bfloat16), part, part),
+        in_specs=[SMEM_SPEC] + [VMEM_SPEC] * 8,
         out_specs=(VMEM_SPEC, VMEM_SPEC, HBM_SPEC, VMEM_SPEC, VMEM_SPEC),
         scratch_shapes=[
             pltpu.SMEM((spans,), jnp.int32),
             pltpu.VMEM((n_rows, dim), jnp.bfloat16),
             pltpu.VMEM(prob.shape, jnp.bfloat16),
-            pltpu.VMEM(prob.shape, jnp.bfloat16),
             pltpu.VMEM((n_rows, LANES), jnp.float32),
             pltpu.VMEM((dim, n_rows), jnp.bfloat16),
-            pltpu.VMEM((dim, n_rows), jnp.bfloat16),
-            pltpu.SemaphoreType.DMA((spans,)),
             pltpu.SemaphoreType.DMA((spans,)),
         ],
-        compiler_params=small_params(VMEM_LIMIT),
+        compiler_params=small_params(BACKWARD_LIMIT),
         name="attend_backward",
-    )(plan, prob, stats_own, stats_mate, acc, q_rows, g_raw, kv_mine, kv_mate)
+    )(plan, prob, stats_own, stats_mate, acc, q_cols, g_raw, kv_mine, kv_mate)
 
 
 def finish_call(plan, ds_rows, kv_mine, kv_mate, group=768):
@@ -445,21 +474,24 @@
             pltpu.VMEM((n_rows, dim), jnp.float32),
             pltpu.SemaphoreType.DMA((spans,)),
         ],
-        compiler_params=small_params(VMEM_LIMIT),
-        cost_estimate=LONG,
+        compiler_params=small_params(BACKWARD_LIMIT),
+        cost_estimate=MEDIUM,
         name="attend_finish",
     )(plan, ds_rows, kv_mine, kv_mate)
 
 
-def spread_call(keys, values, n_z):
+def spread_call(keys, values, queries, n_z):
     tok, dim = keys.shape
     return pl.pallas_call(
         spread,
-        out_shape=jax.ShapeDtypeStruct((n_z, tok, 2 * dim), jnp.bfloat16),
-        in_specs=[VMEM_SPEC] * 2,
-        out_specs=VMEM_SPEC,
+        out_shape=(
+            jax.ShapeDtypeStruct((n_z, tok, 2 * dim), jnp.bfloat16),
+            jax.ShapeDtypeStruct((1, tok), jnp.float32),
+        ),
+        in_specs=[VMEM_SPEC] * 3,
+        out_specs=(VMEM_SPEC,) * 2,
         name="spread",
-    )(keys, values)
+    )(keys, values, queries)
 
 
 def head_sum(x):
@@ -481,26 +513,27 @@
 
     q_mate = lax.ppermute(queries, "xh", SWAP)
     g_mate = lax.ppermute(out_grad, "xh", SWAP)
-    kv_mine = lax.all_to_all(spread_call(key_states, value_states, n_z), "z", 0, 0)
-    square_sum = head_sum(row_squares_call(queries, q_mate))
+    kv_out, own_squares = spread_call(key_states, value_states, queries, n_z)
+    kv_mine = lax.all_to_all(kv_out, "z", 0, 0)
+    square_sum = head_sum(row_squares_call(own_squares, q_mate))
     q_raw, g_raw = prepare_call(queries, q_mate, out_grad, g_mate, dim)
     kv_mine, square_sum, q_raw, g_raw = lax.optimization_barrier(
         (kv_mine, square_sum, q_raw, g_raw)
     )
     kv_mate = lax.ppermute(kv_mine, "core", SWAP)
 
-    prob, acc, stats, q_rows = forward_call(
-        plan, square_sum, norm_gain[None, :], q_raw, g_raw, kv_mine, kv_mate, local * n_heads
-    )
+    q_rows, q_cols = normalize_call(square_sum, norm_gain[None, :], q_raw, local * n_heads)
+    prob, acc, stats = forward_call(plan, q_rows, g_raw, kv_mine, kv_mate)
     stats_mate = lax.ppermute(stats, "xh", SWAP)
     out_keep, out_give, ds_rows, dkv_keep, dkv_give = backward_call(
-        plan, prob, stats, stats_mate, acc, q_rows, g_raw, kv_mine, kv_mate
+        plan, prob, stats, stats_mate, acc, q_cols, g_raw, kv_mine, kv_mate
     )
     out_got = lax.ppermute(out_give, "xh", SWAP)
     dkv_got = lax.ppermute(dkv_give, "core", SWAP)
-    chip = (dkv_keep.astype(jnp.float32) + dkv_got.astype(jnp.float32)).astype(jnp.bfloat16)
+    chip = add_pair_call(dkv_keep, dkv_got)
     chip, ds_rows = lax.optimization_barrier((chip, ds_rows))
     pieces = lax.all_to_all(chip, "z", 0, 0)
+    ds_rows = pltpu.with_memory_space_constraint(ds_rows, pltpu.HBM)
     dq_keep, dq_give = finish_call(plan, ds_rows, kv_mine, kv_mate)
     dq_got = lax.ppermute(dq_give, "xh", SWAP)
     attn_out, d_queries = merge_call(out_keep, out_got, dq_keep, dq_got)

time: 78.3 us -> 74.3 us (0.949)
  Pallas kernels: 19.1 us -> 13.9 us
  starting transfers between devices: 31.5 us -> 32.8 us
  waiting for transfers between devices: 24.5 us -> 25.7 us
  other arithmetic: 1.03 us -> 0.08 us
    pallas_call x1, Pallas kernels: 6.08 us -> 2.84 us  [forward_call(): pl.pallas_call(functools.partial(forward, tok=tok, heads=heads, dim=dim,...]
    all_to_all x1, starting transfers between devices: 3.49 us -> 6.13 us  [shards(): pieces = lax.all_to_all(chip, 'z', 0, 0)]
    pallas_call x1, Pallas kernels: 6.41 us -> 4.09 us  [backward_call(): pl.pallas_call(functools.partial(backward, tok=tok, heads=heads, dim=dim,...]
    ppermute x1, waiting for transfers between devices: 0.01 us -> 1.54 us  [shards(): dkv_got = lax.ppermute(dkv_give, 'core', SWAP)]
    pallas_call x2 -> x4, Pallas kernels: 1.76 us -> 3.27 us  [the longest x1 1.85 us: spread_call(): pl.pallas_call(spread, out_shape=(jax.ShapeDtypeStruct((n_z, tok, 2 * dim...]
    ppermute x1, waiting for transfers between devices: 0.01 us -> 1.48 us  [shards(): out_got = lax.ppermute(out_give, 'xh', SWAP)]
    ppermute x1, starting transfers between devices: 1.6 us -> 0.31 us  [shards(): dq_got = lax.ppermute(dq_give, 'xh', SWAP)]
    pallas_call x1, Pallas kernels: 3.93 us -> 2.75 us  [finish_call(): pl.pallas_call(functools.partial(finish, tok=tok, heads=heads, dim=dim, g...]
  transfers between devices with their start and end apart: 13 -> 13, of which waited for: 8 -> 10; matrix products, arithmetic and copies ran while one was open for 1% -> 0% of each run, Pallas kernels for 8% -> 8%
where the time goes in v1:
time: 74.3 us; the launch traced here: 74.6 us
  starting transfers between devices  32.8 us (44%)
  waiting for transfers between devices  25.7 us (35%)
  Pallas kernels  13.9 us (19%)
  local copies, waits for them, and re-layouts  1.39 us (2%)
    all_to_all x1, starting transfers between devices, shards(): kv_mine = lax.all_to_all(kv_out, 'z', 0, 0)  8.31 us
    all_to_all x1, starting transfers between devices, shards(): pieces = lax.all_to_all(chip, 'z', 0, 0)  6.13 us
    all_to_all x1, waiting for transfers between devices, shards(): kv_mine = lax.all_to_all(kv_out, 'z', 0, 0)  6.06 us
    ppermute x1, waiting for transfers between devices, shards(): dq_got = lax.ppermute(dq_give, 'xh', SWAP)  5.27 us
    all_to_all x1, waiting for transfers between devices, shards(): pieces = lax.all_to_all(chip, 'z', 0, 0)  4.6 us
    pallas_call x1, Pallas kernels, backward_call(): pl.pallas_call(functools.partial(backward, tok=tok, heads=heads, dim=dim,...  4.09 us
    ppermute x3, starting transfers between devices, head_sum(): lax.ppermute(x, 'y', [(i, (i + d) % n) for i in range(n)])  3.77 us
    ppermute x1, starting transfers between devices, shards(): q_mate = lax.ppermute(queries, 'xh', SWAP)  3.66 us
  transfers between devices with their start and end apart: 13, of which 10 were waited for; matrix products, arithmetic and copies ran while one was open for 0% of the time, Pallas kernels for 8%

profile of v1, /device:TPU:1, one launch (start us, length us, event | category | flops | bytes accessed | tf_op | source)
XLA Modules:
  0.0 74.6 jit_solution(7867275693892301080)
XLA Ops:
  0.6 3.7 %collective-permute-start = (bf16[128,768]{1,0:T(8,128)(2,1)}, bf16[128,768]{1,0:T(8,128)(2,1)S(1)}, u32[]{:S(2)}, u32[]{:S(2)}) collective-permute-start(bf16[128,768]{1,0:T(8,128)(2,1)} %queries.3), channel_id=1, source_target_pairs={{0,16},{16,0},{1,17},{17,1},{2,18},{18,2},{3,19},{19,3},{4,20},{20... | collective-permute-start | bytes 589832 | tf_op jit(solution)/shard_map/ppermute | solution.py:514
  4.4 1.9 %spread.1 = (bf16[8,128,256]{2,1,0:T(8,128)(2,1)}, f32[1,128]{1,0:T(1,128)}) custom-call(bf16[128,128]{1,0:T(8,128)(2,1)} %keys.1, bf16[128,128]{1,0:T(8,128)(2,1)} %values.1, bf16[128,768]{1,0:T(8,128)(2,1)} %queries.3), custom_call_target="tpu_custom_call" | custom-call | tf_op jit(solution)/shard_map/spread/pallas_call | solution.py:485
  6.2 8.3 %all-to-all-start = ((bf16[8,128,256]{2,1,0:T(8,128)(2,1)}), bf16[8,128,256]{2,1,0:T(8,128)(2,1)S(1)}, u32[]{:S(2)}, u32[]{:S(2)}) async-start(bf16[8,128,256]{2,1,0:T(8,128)(2,1)} %get-tuple-element.28), calls=%async_computation | async-start | bytes 1048576 | tf_op jit(solution)/shard_map/all_to_all | solution.py:517
  14.6 0.6 copy-done.2
  15.3 0.1 row_squares.1
  15.4 1.3 %collective-permute-start.1 = (f32[2,128]{1,0:T(2,128)S(1)}, f32[2,128]{1,0:T(2,128)S(1)}, u32[]{:S(2)}, u32[]{:S(2)}) collective-permute-start(f32[2,128]{1,0:T(2,128)S(1)} %row_squares.1), channel_id=1, source_target_pairs={{0,1},{1,0},{2,3},{3,2},{4,5},{5,4},{6,7},{7,6},{8,9},{9,8},{10,11... | collective-permute-start | bytes 3080 | tf_op jit(solution)/shard_map/ppermute | solution.py:498
  16.7 1.2 %collective-permute-done.1 = f32[2,128]{1,0:T(2,128)S(1)} collective-permute-done((f32[2,128]{1,0:T(2,128)S(1)}, f32[2,128]{1,0:T(2,128)S(1)}, u32[]{:S(2)}, u32[]{:S(2)}) %collective-permute-start.1) | collective-permute-done | bytes 1056 | tf_op jit(solution)/shard_map/ppermute | solution.py:498
  17.9 2.7 %collective-permute-start.4 = (f32[2,128]{1,0:T(2,128)S(1)}, f32[2,128]{1,0:T(2,128)S(1)}, u32[]{:S(2)}, u32[]{:S(2)}) collective-permute-start(f32[2,128]{1,0:T(2,128)S(1)} %add.12), channel_id=1, source_target_pairs={{0,6},{2,0},{4,2},{6,4},{1,7},{3,1},{5,3},{7,5},{8,14},{10,8},{12,... | collective-permute-start | bytes 3080 | tf_op jit(solution)/shard_map/ppermute | solution.py:500
  20.6 0.3 collective-permute-start.3
  21.0 0.7 collective-permute-start.2
  21.7 0.1 prepare.1
  21.8 3.0 %collective-permute-done.3 = f32[2,128]{1,0:T(2,128)S(1)} collective-permute-done((f32[2,128]{1,0:T(2,128)S(1)}, f32[2,128]{1,0:T(2,128)S(1)}, u32[]{:S(2)}, u32[]{:S(2)}) %collective-permute-start.3) | collective-permute-done | bytes 1056 | tf_op jit(solution)/shard_map/ppermute | solution.py:500
  24.9 6.1 %all-to-all-done.kv_mine = bf16[8,128,256]{2,1,0:T(8,128)(2,1)S(1)} async-done(((bf16[8,128,256]{2,1,0:T(8,128)(2,1)}), bf16[8,128,256]{2,1,0:T(8,128)(2,1)S(1)}, u32[]{:S(2)}, u32[]{:S(2)}) %all-to-all-start) | async-done | bytes 524320 | tf_op jit(solution)/shard_map/all_to_all | solution.py:517
  31.0 2.0 %collective-permute-start.6 = (bf16[8,128,256]{2,1,0:T(8,128)(2,1)S(1)}, bf16[8,128,256]{2,1,0:T(8,128)(2,1)S(1)}, u32[]{:S(2)}, u32[]{:S(2)}) collective-permute-start(bf16[8,128,256]{2,1,0:T(8,128)(2,1)S(1)} %all-to-all-done.kv_mine), channel_id=1, source_target_pairs={{0,8},{8,0},{1,9},{9,1},{2,10},{10,2},{3,11},{11,3},{4,12},{12,4},... | collective-permute-start | bytes 1572872 | tf_op jit(solution)/shard_map/ppermute | solution.py:523
  33.1 0.4 normalize.1
  33.5 1.0 %collective-permute-done.6.kv_mate = bf16[8,128,256]{2,1,0:T(8,128)(2,1)S(1)} collective-permute-done((bf16[8,128,256]{2,1,0:T(8,128)(2,1)S(1)}, bf16[8,128,256]{2,1,0:T(8,128)(2,1)S(1)}, u32[]{:S(2)}, u32[]{:S(2)}) %collective-permute-start.6) | collective-permute-done | bytes 524320 | tf_op jit(solution)/shard_map/ppermute | solution.py:523
  34.5 2.8 %attend_forward.1 = (bf16[8,1536,256]{2,1,0:T(8,128)(2,1)S(1)}, f32[1536,128]{1,0:T(8,128)S(1)}, f32[48,128]{1,0:T(8,128)S(1)}) custom-call(s32[27]{0:T(128)S(1)} %concatenate.3.plan, bf16[1536,128]{1,0:T(8,128)(2,1)S(1)} %get-tuple-element.34.q_rows, bf16[1536,128]{1,0:T(8,128)(2,1)S(1)} %get-tuple-element.35.g_raw, ...), custom_call_target="tpu_custom_call" | custom-call | tf_op jit(solution)/shard_map/attend_forward/pallas_call | solution.py:416
  37.4 2.8 %collective-permute-start.7 = (f32[48,128]{1,0:T(8,128)S(1)}, f32[48,128]{1,0:T(8,128)S(1)}, u32[]{:S(2)}, u32[]{:S(2)}) collective-permute-start(f32[48,128]{1,0:T(8,128)S(1)} %get-tuple-element.38.stats_own), channel_id=1, source_target_pairs={{0,16},{16,0},{1,17},{17,1},{2,18},{18,2},{3,19},{19,3},{4,20},{20... | collective-permute-start | bytes 73736 | tf_op jit(solution)/shard_map/ppermute | solution.py:527
  40.2 1.4 %collective-permute-done.7.stats_mate = f32[48,128]{1,0:T(8,128)S(1)} collective-permute-done((f32[48,128]{1,0:T(8,128)S(1)}, f32[48,128]{1,0:T(8,128)S(1)}, u32[]{:S(2)}, u32[]{:S(2)}) %collective-permute-start.7) | collective-permute-done | bytes 24608 | tf_op jit(solution)/shard_map/ppermute | solution.py:527
  41.6 4.1 %attend_backward.1 = (bf16[128,768]{1,0:T(8,128)(2,1)S(1)}, bf16[128,768]{1,0:T(8,128)(2,1)S(1)}, bf16[8,1536,256]{2,1,0:T(8,128)(2,1)}, bf16[8,128,256]{2,1,0:T(8,128)(2,1)S(1)}, bf16[8,128,256]{2,1,0:T(8,128)(2,1)S(1)}) custom-call(s32[27]{0:T(128)S(1)} %concatenate.3.plan, bf16[8,1536,256]{2,1,0:T(8,128)(2,1)S(1)} %get-tuple-element.37.prob, ...), custom_call_target="tpu_custom_call" | custom-call | tf_op jit(solution)/shard_map/attend_backward/pallas_call | solution.py:442
  45.7 1.6 %collective-permute-start.9 = (bf16[8,128,256]{2,1,0:T(8,128)(2,1)S(1)}, bf16[8,128,256]{2,1,0:T(8,128)(2,1)S(1)}, u32[]{:S(2)}, u32[]{:S(2)}) collective-permute-start(bf16[8,128,256]{2,1,0:T(8,128)(2,1)S(1)} %get-tuple-element.44), channel_id=1, source_target_pairs={{0,8},{8,0},{1,9},{9,1},{2,10},{10,2},{3,11},{11,3},{4,12},{12,4},... | collective-permute-start | bytes 1572872 | tf_op jit(solution)/shard_map/ppermute | solution.py:532
  47.3 1.5 %collective-permute-done.9.other = bf16[8,128,256]{2,1,0:T(8,128)(2,1)S(1)} collective-permute-done((bf16[8,128,256]{2,1,0:T(8,128)(2,1)S(1)}, bf16[8,128,256]{2,1,0:T(8,128)(2,1)S(1)}, u32[]{:S(2)}, u32[]{:S(2)}) %collective-permute-start.9) | collective-permute-done | bytes 524320 | tf_op jit(solution)/shard_map/ppermute | solution.py:532
  48.9 0.9 %add_pair.1 = bf16[8,128,256]{2,1,0:T(8,128)(2,1)} custom-call(bf16[8,128,256]{2,1,0:T(8,128)(2,1)S(1)} %get-tuple-element.43.one, bf16[8,128,256]{2,1,0:T(8,128)(2,1)S(1)} %collective-permute-done.9.other), custom_call_target="tpu_custom_call" | custom-call | tf_op jit(solution)/shard_map/add_pair/pallas_call | solution.py:390
  49.8 6.1 %all-to-all-start.1 = ((bf16[8,128,256]{2,1,0:T(8,128)(2,1)}), bf16[8,128,256]{2,1,0:T(8,128)(2,1)S(1)}, u32[]{:S(2)}, u32[]{:S(2)}) async-start(bf16[8,128,256]{2,1,0:T(8,128)(2,1)} %add_pair.1), calls=%async_computation.1 | async-start | bytes 1048576 | tf_op jit(solution)/shard_map/all_to_all | solution.py:535
  55.9 2.7 %collective-permute-start.8 = (bf16[128,768]{1,0:T(8,128)(2,1)S(1)}, bf16[128,768]{1,0:T(8,128)(2,1)S(1)}, u32[]{:S(2)}, u32[]{:S(2)}) collective-permute-start(bf16[128,768]{1,0:T(8,128)(2,1)S(1)} %get-tuple-element.42), channel_id=1, source_target_pairs={{0,16},{16,0},{1,17},{17,1},{2,18},{18,2},{3,19},{19,3},{4,20},{20... | collective-permute-start | bytes 589832 | tf_op jit(solution)/shard_map/ppermute | solution.py:531
  58.7 2.8 %attend_finish.1 = (bf16[128,768]{1,0:T(8,128)(2,1)S(1)}, bf16[128,768]{1,0:T(8,128)(2,1)S(1)}) custom-call(s32[27]{0:T(128)S(1)} %concatenate.3.plan, bf16[8,1536,256]{2,1,0:T(8,128)(2,1)} %get-tuple-element.46.ds_in, bf16[8,128,256]{2,1,0:T(8,128)(2,1)S(1)} %all-to-all-done.kv_mine, bf16[8,128,256]{2,1,0:T(8,128)(2,1)S(1)} %collective-permute-done.6.kv_mate), custom_call_target="tpu_custom_call" | custom-call | flops 3000000000 | bytes 1024 | tf_op jit(solution)/shard_map/attend_finish/pallas_call | solution.py:466
  61.4 0.3 collective-permute-start.10
  61.7 1.5 %collective-permute-done.8.out_got = bf16[128,768]{1,0:T(8,128)(2,1)S(1)} collective-permute-done((bf16[128,768]{1,0:T(8,128)(2,1)S(1)}, bf16[128,768]{1,0:T(8,128)(2,1)S(1)}, u32[]{:S(2)}, u32[]{:S(2)}) %collective-permute-start.8) | collective-permute-done | bytes 196640 | tf_op jit(solution)/shard_map/ppermute | solution.py:531
  63.2 5.3 %collective-permute-done.10.dq_got = bf16[128,768]{1,0:T(8,128)(2,1)S(1)} collective-permute-done((bf16[128,768]{1,0:T(8,128)(2,1)S(1)}, bf16[128,768]{1,0:T(8,128)(2,1)S(1)}, u32[]{:S(2)}, u32[]{:S(2)}) %collective-permute-start.10) | collective-permute-done | bytes 196640 | tf_op jit(solution)/shard_map/ppermute | solution.py:538
  68.5 0.8 %merge.1 = (bf16[128,768]{1,0:T(8,128)(2,1)}, bf16[128,768]{1,0:T(8,128)(2,1)}) custom-call(bf16[128,768]{1,0:T(8,128)(2,1)S(1)} %get-tuple-element.41.out_keep, bf16[128,768]{1,0:T(8,128)(2,1)S(1)} %collective-permute-done.8.out_got, bf16[128,768]{1,0:T(8,128)(2,1)S(1)} %get-tuple-element.47.dq_keep, bf16[128,768]{1,0:T(8,128)(2,1)S(1)} %collective-permute-done.10.dq_got), custom_call_target="tpu_custom_call" | custom-call | flops 1024 | bytes 1024 | tf_op jit(solution)/shard_map/merge/pallas_call | solution.py:402
  69.3 4.6 %all-to-all-done.1 = bf16[8,128,256]{2,1,0:T(8,128)(2,1)S(1)} async-done(((bf16[8,128,256]{2,1,0:T(8,128)(2,1)}), bf16[8,128,256]{2,1,0:T(8,128)(2,1)S(1)}, u32[]{:S(2)}, u32[]{:S(2)}) %all-to-all-start.1) | async-done | bytes 524320 | tf_op jit(solution)/shard_map/all_to_all | solution.py:535
  74.0 0.6 fusion
  (23 shorter events, 0.4 us)
Async XLA Ops:
  0.6 13.9 %collective-permute-start = (bf16[128,768]{1,0:T(8,128)(2,1)}, bf16[128,768]{1,0:T(8,128)(2,1)S(1)}, u32[]{:S(2)}, u32[]{:S(2)}) collective-permute-start(bf16[128,768]{1,0:T(8,128)(2,1)} %queries.3), channel_id=1, source_target_pairs={{0,16},{16,0},{1,17},{17,1},{2,18},{18,2},{3,19},{19,3},{4,20},{20... | collective-permute-start | bytes 589832 | tf_op jit(solution)/shard_map/ppermute | solution.py:514
  4.3 17.4 %collective-permute-start.5 = (bf16[128,768]{1,0:T(8,128)(2,1)}, bf16[128,768]{1,0:T(8,128)(2,1)S(1)}, u32[]{:S(2)}, u32[]{:S(2)}) collective-permute-start(bf16[128,768]{1,0:T(8,128)(2,1)} %out_grad.1), channel_id=1, source_target_pairs={{0,16},{16,0},{1,17},{17,1},{2,18},{18,2},{3,19},{19,3},{4,20},{20... | collective-permute-start | bytes 589832 | tf_op jit(solution)/shard_map/ppermute | solution.py:515
  6.2 24.7 %all-to-all-start = ((bf16[8,128,256]{2,1,0:T(8,128)(2,1)}), bf16[8,128,256]{2,1,0:T(8,128)(2,1)S(1)}, u32[]{:S(2)}, u32[]{:S(2)}) async-start(bf16[8,128,256]{2,1,0:T(8,128)(2,1)} %get-tuple-element.28), calls=%async_computation | async-start | bytes 1048576 | tf_op jit(solution)/shard_map/all_to_all | solution.py:517
  14.6 0.7 copy-start.2
  15.2 6.4 %copy-start = (bf16[128,768]{1,0:T(8,128)(2,1)S(1)}, bf16[128,768]{1,0:T(8,128)(2,1)}, u32[]{:S(2)}) copy-start(bf16[128,768]{1,0:T(8,128)(2,1)} %queries.3) | copy-start | bytes 589828
  15.2 6.4 %copy-start.1 = (bf16[128,768]{1,0:T(8,128)(2,1)S(1)}, bf16[128,768]{1,0:T(8,128)(2,1)}, u32[]{:S(2)}) copy-start(bf16[128,768]{1,0:T(8,128)(2,1)} %out_grad.1) | copy-start | bytes 589828
  15.2 17.8 %copy-start.3 = (f32[768]{0:T(1024)S(1)}, f32[768]{0:T(1024)}, u32[]{:S(2)}) copy-start(f32[768]{0:T(1024)} %param.12) | copy-start | bytes 9220
  15.2 17.8 %copy-start.4 = (s32[8]{0:T(128)S(1)}, s32[8]{0:T(128)}, u32[]{:S(2)}) copy-start(s32[8]{0:T(128)} %param.13) | copy-start | bytes 100
  15.2 17.8 %copy-start.5 = (s32[8]{0:T(128)S(1)}, s32[8]{0:T(128)}, u32[]{:S(2)}) copy-start(s32[8]{0:T(128)} %param.14) | copy-start | bytes 100
  15.2 17.8 %copy-start.6 = (s32[8]{0:T(128)S(1)}, s32[8]{0:T(128)}, u32[]{:S(2)}) copy-start(s32[8]{0:T(128)} %param.15) | copy-start | bytes 100
  15.4 2.5 %collective-permute-start.1 = (f32[2,128]{1,0:T(2,128)S(1)}, f32[2,128]{1,0:T(2,128)S(1)}, u32[]{:S(2)}, u32[]{:S(2)}) collective-permute-start(f32[2,128]{1,0:T(2,128)S(1)} %row_squares.1), channel_id=1, source_target_pairs={{0,1},{1,0},{2,3},{3,2},{4,5},{5,4},{6,7},{7,6},{8,9},{9,8},{10,11... | collective-permute-start | bytes 3080 | tf_op jit(solution)/shard_map/ppermute | solution.py:498
  17.9 3.9 %collective-permute-start.4 = (f32[2,128]{1,0:T(2,128)S(1)}, f32[2,128]{1,0:T(2,128)S(1)}, u32[]{:S(2)}, u32[]{:S(2)}) collective-permute-start(f32[2,128]{1,0:T(2,128)S(1)} %add.12), channel_id=1, source_target_pairs={{0,6},{2,0},{4,2},{6,4},{1,7},{3,1},{5,3},{7,5},{8,14},{10,8},{12,... | collective-permute-start | bytes 3080 | tf_op jit(solution)/shard_map/ppermute | solution.py:500
  20.6 4.2 %collective-permute-start.3 = (f32[2,128]{1,0:T(2,128)S(1)}, f32[2,128]{1,0:T(2,128)S(1)}, u32[]{:S(2)}, u32[]{:S(2)}) collective-permute-start(f32[2,128]{1,0:T(2,128)S(1)} %add.12), channel_id=1, source_target_pairs={{0,4},{2,6},{4,0},{6,2},{1,5},{3,7},{5,1},{7,3},{8,12},{10,14},{12... | collective-permute-start | bytes 3080 | tf_op jit(solution)/shard_map/ppermute | solution.py:500
  21.0 3.9 %collective-permute-start.2 = (f32[2,128]{1,0:T(2,128)S(1)}, f32[2,128]{1,0:T(2,128)S(1)}, u32[]{:S(2)}, u32[]{:S(2)}) collective-permute-start(f32[2,128]{1,0:T(2,128)S(1)} %add.12), channel_id=1, source_target_pairs={{0,2},{2,4},{4,6},{6,0},{1,3},{3,5},{5,7},{7,1},{8,10},{10,12},{12... | collective-permute-start | bytes 3080 | tf_op jit(solution)/shard_map/ppermute | solution.py:500
  31.0 3.6 %collective-permute-start.6 = (bf16[8,128,256]{2,1,0:T(8,128)(2,1)S(1)}, bf16[8,128,256]{2,1,0:T(8,128)(2,1)S(1)}, u32[]{:S(2)}, u32[]{:S(2)}) collective-permute-start(bf16[8,128,256]{2,1,0:T(8,128)(2,1)S(1)} %all-to-all-done.kv_mine), channel_id=1, source_target_pairs={{0,8},{8,0},{1,9},{9,1},{2,10},{10,2},{3,11},{11,3},{4,12},{12,4},... | collective-permute-start | bytes 1572872 | tf_op jit(solution)/shard_map/ppermute | solution.py:523
  37.4 4.2 %collective-permute-start.7 = (f32[48,128]{1,0:T(8,128)S(1)}, f32[48,128]{1,0:T(8,128)S(1)}, u32[]{:S(2)}, u32[]{:S(2)}) collective-permute-start(f32[48,128]{1,0:T(8,128)S(1)} %get-tuple-element.38.stats_own), channel_id=1, source_target_pairs={{0,16},{16,0},{1,17},{17,1},{2,18},{18,2},{3,19},{19,3},{4,20},{20... | collective-permute-start | bytes 73736 | tf_op jit(solution)/shard_map/ppermute | solution.py:527
  45.7 3.1 %collective-permute-start.9 = (bf16[8,128,256]{2,1,0:T(8,128)(2,1)S(1)}, bf16[8,128,256]{2,1,0:T(8,128)(2,1)S(1)}, u32[]{:S(2)}, u32[]{:S(2)}) collective-permute-start(bf16[8,128,256]{2,1,0:T(8,128)(2,1)S(1)} %get-tuple-element.44), channel_id=1, source_target_pairs={{0,8},{8,0},{1,9},{9,1},{2,10},{10,2},{3,11},{11,3},{4,12},{12,4},... | collective-permute-start | bytes 1572872 | tf_op jit(solution)/shard_map/ppermute | solution.py:532
  49.8 24.1 %all-to-all-start.1 = ((bf16[8,128,256]{2,1,0:T(8,128)(2,1)}), bf16[8,128,256]{2,1,0:T(8,128)(2,1)S(1)}, u32[]{:S(2)}, u32[]{:S(2)}) async-start(bf16[8,128,256]{2,1,0:T(8,128)(2,1)} %add_pair.1), calls=%async_computation.1 | async-start | bytes 1048576 | tf_op jit(solution)/shard_map/all_to_all | solution.py:535
  55.9 7.3 %collective-permute-start.8 = (bf16[128,768]{1,0:T(8,128)(2,1)S(1)}, bf16[128,768]{1,0:T(8,128)(2,1)S(1)}, u32[]{:S(2)}, u32[]{:S(2)}) collective-permute-start(bf16[128,768]{1,0:T(8,128)(2,1)S(1)} %get-tuple-element.42), channel_id=1, source_target_pairs={{0,16},{16,0},{1,17},{17,1},{2,18},{18,2},{3,19},{19,3},{4,20},{20... | collective-permute-start | bytes 589832 | tf_op jit(solution)/shard_map/ppermute | solution.py:531
  61.4 7.1 %collective-permute-start.10 = (bf16[128,768]{1,0:T(8,128)(2,1)S(1)}, bf16[128,768]{1,0:T(8,128)(2,1)S(1)}, u32[]{:S(2)}, u32[]{:S(2)}) collective-permute-start(bf16[128,768]{1,0:T(8,128)(2,1)S(1)} %get-tuple-element.48), channel_id=1, source_target_pairs={{0,16},{16,0},{1,17},{17,1},{2,18},{18,2},{3,19},{19,3},{4,20},{20... | collective-permute-start | bytes 589832 | tf_op jit(solution)/shard_map/ppermute | solution.py:538

commit v2 on v1

--- a/solution.py
+++ b/solution.py
@@ -15,13 +15,14 @@
 LN2 = 0.6931471805599453
 LANES = 128
 STATS = 3
+STAT_ROWS = 16
 
 CTX = ("z", "xh", "core")
 HEAD = ("y", "xl")
 SWAP = [(0, 1), (1, 0)]
 VMEM_LIMIT = 24 * 2**20
 BACKWARD_LIMIT = 18 * 2**20
-SMALL_LIMIT = 8 * 2**20
+SMALL_LIMIT = 9 * 2**20
 LONG = pl.CostEstimate(flops=2 * 10**10, bytes_accessed=2**20, transcendentals=0)
 MEDIUM = pl.CostEstimate(flops=3 * 10**9, bytes_accessed=2**10, transcendentals=0)
 SHORT = pl.CostEstimate(flops=2**10, bytes_accessed=2**10, transcendentals=0)
@@ -202,9 +203,9 @@
     for j in range(2 * heads):
         r = slice(j * tok, (j + 1) * tok)
         grad = g_raw[r, :].astype(jnp.float32)
-        table = jnp.where(lane == STATS * j, row_max[r, :], table)
-        table = jnp.where(lane == STATS * j + 1, lane_sum(row_sum[r, :]), table)
-        table = jnp.where(lane == STATS * j + 2, lane_sum(grad * acc[r, :]), table)
+        columns = (row_max[r, :], lane_sum(row_sum[r, :]), lane_sum(grad * acc[r, :]))
+        for k, column in enumerate(columns):
+            table = jnp.where(lane == STAT_ROWS * k + j, column, table)
     stats[...] = jnp.transpose(table)[: stats.shape[0], :]
 
 
@@ -218,18 +219,28 @@
     count, _ = visible_slots(plan, order, spans)
 
     half = heads * tok
-    mine, theirs = columns_of(stats_own[...]), columns_of(stats_mate[...])
+    def parts_of(stats):
+        return [stats[k * STAT_ROWS : (k + 1) * STAT_ROWS, :] for k in range(STATS)]
+
+    def partner(x):
+        return jnp.concatenate([x[heads : 2 * heads], x[:heads], x[2 * heads :]], axis=0)
+
+    top_mine, sum_mine, delta_mine = parts_of(stats_own[...])
+    top_other, sum_other, delta_other = [partner(x) for x in parts_of(stats_mate[...])]
+    top = jnp.maximum(top_mine, top_other)
+    f_mine, f_other = jnp.exp2(top_mine - top), jnp.exp2(top_other - top)
+    total = sum_mine * f_mine + sum_other * f_other
+    used = lax.broadcasted_iota(jnp.int32, total.shape, 0) < 2 * heads
+    total = jnp.where(used, total, 1.0)
+    scales = f_mine / total
+    deltas = (delta_mine * f_mine + delta_other * f_other) / total * scales
+    columns = columns_of(jnp.concatenate([scales, deltas], axis=0))
     for j in range(2 * heads):
         r = slice(j * tok, (j + 1) * tok)
         h = slice((j % heads) * dim, (j % heads + 1) * dim)
-        a, b = STATS * j, STATS * ((j + heads) % (2 * heads))
-        top = jnp.maximum(mine[:, a : a + 1], theirs[:, b : b + 1])
-        f_mine = jnp.exp2(mine[:, a : a + 1] - top)
-        f_theirs = jnp.exp2(theirs[:, b : b + 1] - top)
-        total = mine[:, a + 1 : a + 2] * f_mine + theirs[:, b + 1 : b + 2] * f_theirs
-        scale = f_mine / total
-        delta = (mine[:, a + 2 : a + 3] * f_mine + theirs[:, b + 2 : b + 3] * f_theirs) / total
-        delta_rows[r, :] = jnp.broadcast_to(delta * scale, (tok, LANES))
+        scale = columns[:, j : j + 1]
+        delta = columns[:, STAT_ROWS + j : STAT_ROWS + j + 1]
+        delta_rows[r, :] = jnp.broadcast_to(delta, (tok, LANES))
         out = out_keep if j < heads else out_give
         g_rows[r, :] = (g_raw[r, :].astype(jnp.float32) * scale).astype(jnp.bfloat16)
         out[:, h] = (acc_in[r, :] * scale).astype(jnp.bfloat16)
@@ -284,34 +295,33 @@
 
 
 def finish(
-    plan, ds_in, kv_mine, kv_mate, dq_keep, dq_give, order, ds_rows, acc, sems,
-    *, tok, heads, dim, group,
+    plan, ds_in, kv_mine, kv_mate, d_queries, order, ds_rows, acc, sems,
+    *, tok, heads, dim, first_row,
 ):
     count, _ = visible_slots(plan, order, order.shape[0])
+    n_rows = heads * tok
+
+    def fetch(b):
+        source = ds_in.at[b, pl.ds(first_row, n_rows)]
+        return pltpu.make_async_copy(source, ds_rows.at[b], sems.at[b])
 
     @pl.loop(0, count)
     def _(b):
-        pltpu.make_async_copy(ds_in.at[b], ds_rows.at[b], sems.at[b]).start()
-
-
-    half = heads * tok
-    chunks = [slice(r, r + group) for r in range(0, 2 * half, group)]
+        fetch(b).start()
+
     acc[...] = jnp.zeros_like(acc)
 
     def add(first, n):
         keys = stacked(order, first, n, slice(0, dim), kv_mine, kv_mate)
         for k in range(n):
-            b = first + k
-            pltpu.make_async_copy(ds_in.at[b], ds_rows.at[b], sems.at[b]).wait()
-        for c in chunks:
-            ds = jnp.concatenate([ds_rows[first + k, c, :] for k in range(n)], axis=1)
-            acc[c, :] += dot(ds, keys)
+            fetch(first + k).wait()
+        ds = jnp.concatenate([ds_rows[first + k] for k in range(n)], axis=1)
+        acc[...] += dot(ds, keys)
 
     by_pairs(count, add)
-    for j in range(2 * heads):
-        h = slice((j % heads) * dim, (j % heads + 1) * dim)
-        dq = dq_keep if j < heads else dq_give
-        dq[:, h] = (acc[j * tok : (j + 1) * tok, :] / math.sqrt(dim)).astype(jnp.bfloat16)
+    for h in range(heads):
+        rows_of = acc[h * tok : (h + 1) * tok, :] / math.sqrt(dim)
+        d_queries[:, h * dim : (h + 1) * dim] = rows_of.astype(jnp.bfloat16)
 
 
 def spread(keys, values, queries, out, squares):
@@ -412,13 +422,12 @@
 
 def forward_call(plan, q_rows, g_raw, kv_mine, kv_mate, group=384):
     spans, tok, dim, heads, n_rows = sizes_of(q_rows, kv_mine)
-    stat_rows = -(-2 * heads * STATS // 16) * 16
     return pl.pallas_call(
         functools.partial(forward, tok=tok, heads=heads, dim=dim, group=group),
         out_shape=(
             jax.ShapeDtypeStruct((spans, n_rows, 2 * tok), jnp.bfloat16),
             jax.ShapeDtypeStruct((n_rows, dim), jnp.float32),
-            jax.ShapeDtypeStruct((stat_rows, LANES), jnp.float32),
+            jax.ShapeDtypeStruct((STATS * STAT_ROWS, LANES), jnp.float32),
         ),
         in_specs=[SMEM_SPEC] + [VMEM_SPEC] * 4,
         out_specs=(VMEM_SPEC,) * 3,
@@ -457,26 +466,27 @@
     )(plan, prob, stats_own, stats_mate, acc, q_cols, g_raw, kv_mine, kv_mate)
 
 
-def finish_call(plan, ds_rows, kv_mine, kv_mate, group=768):
-    spans, n_rows, _ = ds_rows.shape
+def finish_call(plan, ds_rows, kv_mine, kv_mate, side, cost):
+    ds_rows = pltpu.with_memory_space_constraint(ds_rows, pltpu.HBM)
+    spans, n_rows, n_keys = ds_rows.shape
     _, tok, both = kv_mine.shape
     dim = both // 2
-    heads = n_rows // (2 * tok)
-    rows = jax.ShapeDtypeStruct((tok, heads * dim), jnp.bfloat16)
-    return pl.pallas_call(
-        functools.partial(finish, tok=tok, heads=heads, dim=dim, group=group),
-        out_shape=(rows, rows),
+    half = n_rows // 2
+    heads = half // tok
+    return pl.pallas_call(
+        functools.partial(finish, tok=tok, heads=heads, dim=dim, first_row=side * half),
+        out_shape=jax.ShapeDtypeStruct((tok, heads * dim), jnp.bfloat16),
         in_specs=[SMEM_SPEC, HBM_SPEC, VMEM_SPEC, VMEM_SPEC],
-        out_specs=(VMEM_SPEC,) * 2,
+        out_specs=VMEM_SPEC,
         scratch_shapes=[
             pltpu.SMEM((spans,), jnp.int32),
-            pltpu.VMEM(ds_rows.shape, jnp.bfloat16),
-            pltpu.VMEM((n_rows, dim), jnp.float32),
+            pltpu.VMEM((spans, half, n_keys), jnp.bfloat16),
+            pltpu.VMEM((half, dim), jnp.float32),
             pltpu.SemaphoreType.DMA((spans,)),
         ],
-        compiler_params=small_params(BACKWARD_LIMIT),
-        cost_estimate=MEDIUM,
-        name="attend_finish",
+        compiler_params=small_params(),
+        cost_estimate=cost,
+        name=("finish_own", "finish_mate")[side],
     )(plan, ds_rows, kv_mine, kv_mate)
 
 
@@ -533,9 +543,10 @@
     chip = add_pair_call(dkv_keep, dkv_got)
     chip, ds_rows = lax.optimization_barrier((chip, ds_rows))
     pieces = lax.all_to_all(chip, "z", 0, 0)
-    ds_rows = pltpu.with_memory_space_constraint(ds_rows, pltpu.HBM)
-    dq_keep, dq_give = finish_call(plan, ds_rows, kv_mine, kv_mate)
+    dq_give = finish_call(plan, ds_rows, kv_mine, kv_mate, 1, MEDIUM)
     dq_got = lax.ppermute(dq_give, "xh", SWAP)
+    ds_rows, _ = lax.optimization_barrier((ds_rows, dq_give))
+    dq_keep = finish_call(plan, ds_rows, kv_mine, kv_mate, 0, MEDIUM)
     attn_out, d_queries = merge_call(out_keep, out_got, dq_keep, dq_got)
     total = jnp.sum(pieces.astype(jnp.float32), axis=0).astype(jnp.bfloat16)
     return (attn_out, d_queries, total[:, :dim], total[:, dim:])

time: 74.3 us -> 73.5 us (0.989)
  Pallas kernels: 13.9 us -> 16.3 us
  waiting for transfers between devices: 25.7 us -> 23.4 us
  starting transfers between devices: 32.8 us -> 31.2 us
    pallas_call x1 -> x2, Pallas kernels: 2.75 us -> 5.03 us  [finish_call(): pl.pallas_call(functools.partial(finish, tok=tok, heads=heads, dim=dim, f...]
    all_to_all x1, starting transfers between devices: 6.13 us -> 4.54 us  [shards(): pieces = lax.all_to_all(chip, 'z', 0, 0)]
    ppermute x1, waiting for transfers between devices: 1.48 us -> 0.01 us  [shards(): out_got = lax.ppermute(out_give, 'xh', SWAP)]
    ppermute x1, waiting for transfers between devices: 5.27 us -> 4.22 us  [shards(): dq_got = lax.ppermute(dq_give, 'xh', SWAP)]
  transfers between devices with their start and end apart: 13 -> 13, of which waited for: 10 -> 9; matrix products, arithmetic and copies ran while one was open for 0% -> 0% of each run, Pallas kernels for 8% -> 11%
where the time goes in v2:
time: 73.5 us; the launch traced here: 73.2 us
  starting transfers between devices  31.2 us (42%)
  waiting for transfers between devices  23.4 us (32%)
  Pallas kernels  16.3 us (22%)
  local copies, waits for them, and re-layouts  1.39 us (2%)
  between operations  0.76 us (1%)
    all_to_all x1, starting transfers between devices, shards(): kv_mine = lax.all_to_all(kv_out, 'z', 0, 0)  8.31 us
    all_to_all x1, waiting for transfers between devices, shards(): kv_mine = lax.all_to_all(kv_out, 'z', 0, 0)  6.06 us
    pallas_call x2, Pallas kernels, finish_call(): pl.pallas_call(functools.partial(finish, tok=tok, heads=heads, dim=dim, f...  5.03 us
    all_to_all x1, waiting for transfers between devices, shards(): pieces = lax.all_to_all(chip, 'z', 0, 0)  4.84 us
    all_to_all x1, starting transfers between devices, shards(): pieces = lax.all_to_all(chip, 'z', 0, 0)  4.54 us
    ppermute x1, waiting for transfers between devices, shards(): dq_got = lax.ppermute(dq_give, 'xh', SWAP)  4.22 us
    ppermute x3, starting transfers between devices, head_sum(): lax.ppermute(x, 'y', [(i, (i + d) % n) for i in range(n)])  3.77 us
    pallas_call x1, Pallas kernels, backward_call(): pl.pallas_call(functools.partial(backward, tok=tok, heads=heads, dim=dim,...  3.68 us
  transfers between devices with their start and end apart: 13, of which 9 were waited for; matrix products, arithmetic and copies ran while one was open for 0% of the time, Pallas kernels for 11%

profile of v2, /device:TPU:1, one launch (start us, length us, event | category | flops | bytes accessed | tf_op | source)
XLA Modules:
  0.0 73.2 jit_solution(10081100017247724460)
XLA Ops:
  0.6 3.7 %collective-permute-start = (bf16[128,768]{1,0:T(8,128)(2,1)}, bf16[128,768]{1,0:T(8,128)(2,1)S(1)}, u32[]{:S(2)}, u32[]{:S(2)}) collective-permute-start(bf16[128,768]{1,0:T(8,128)(2,1)} %queries.3), channel_id=1, source_target_pairs={{0,16},{16,0},{1,17},{17,1},{2,18},{18,2},{3,19},{19,3},{4,20},{20... | collective-permute-start | bytes 589832 | tf_op jit(solution)/shard_map/ppermute | solution.py:524
  4.4 1.8 %spread.1 = (bf16[8,128,256]{2,1,0:T(8,128)(2,1)}, f32[1,128]{1,0:T(1,128)}) custom-call(bf16[128,128]{1,0:T(8,128)(2,1)} %keys.1, bf16[128,128]{1,0:T(8,128)(2,1)} %values.1, bf16[128,768]{1,0:T(8,128)(2,1)} %queries.3), custom_call_target="tpu_custom_call" | custom-call | tf_op jit(solution)/shard_map/spread/pallas_call | solution.py:495
  6.2 8.3 %all-to-all-start = ((bf16[8,128,256]{2,1,0:T(8,128)(2,1)}), bf16[8,128,256]{2,1,0:T(8,128)(2,1)S(1)}, u32[]{:S(2)}, u32[]{:S(2)}) async-start(bf16[8,128,256]{2,1,0:T(8,128)(2,1)} %get-tuple-element.27), calls=%async_computation | async-start | bytes 1048576 | tf_op jit(solution)/shard_map/all_to_all | solution.py:527
  14.6 0.6 copy-done.2
  15.2 0.1 row_squares.1
  15.4 1.3 %collective-permute-start.1 = (f32[2,128]{1,0:T(2,128)S(1)}, f32[2,128]{1,0:T(2,128)S(1)}, u32[]{:S(2)}, u32[]{:S(2)}) collective-permute-start(f32[2,128]{1,0:T(2,128)S(1)} %row_squares.1), channel_id=1, source_target_pairs={{0,1},{1,0},{2,3},{3,2},{4,5},{5,4},{6,7},{7,6},{8,9},{9,8},{10,11... | collective-permute-start | bytes 3080 | tf_op jit(solution)/shard_map/ppermute | solution.py:508
  16.7 1.2 %collective-permute-done.1 = f32[2,128]{1,0:T(2,128)S(1)} collective-permute-done((f32[2,128]{1,0:T(2,128)S(1)}, f32[2,128]{1,0:T(2,128)S(1)}, u32[]{:S(2)}, u32[]{:S(2)}) %collective-permute-start.1) | collective-permute-done | bytes 1056 | tf_op jit(solution)/shard_map/ppermute | solution.py:508
  17.9 2.7 %collective-permute-start.4 = (f32[2,128]{1,0:T(2,128)S(1)}, f32[2,128]{1,0:T(2,128)S(1)}, u32[]{:S(2)}, u32[]{:S(2)}) collective-permute-start(f32[2,128]{1,0:T(2,128)S(1)} %add.12), channel_id=1, source_target_pairs={{0,6},{2,0},{4,2},{6,4},{1,7},{3,1},{5,3},{7,5},{8,14},{10,8},{12,... | collective-permute-start | bytes 3080 | tf_op jit(solution)/shard_map/ppermute | solution.py:510
  20.6 0.3 collective-permute-start.3
  20.9 0.7 collective-permute-start.2
  21.7 0.1 prepare.1
  21.8 3.0 %collective-permute-done.3 = f32[2,128]{1,0:T(2,128)S(1)} collective-permute-done((f32[2,128]{1,0:T(2,128)S(1)}, f32[2,128]{1,0:T(2,128)S(1)}, u32[]{:S(2)}, u32[]{:S(2)}) %collective-permute-start.3) | collective-permute-done | bytes 1056 | tf_op jit(solution)/shard_map/ppermute | solution.py:510
  24.9 6.1 %all-to-all-done.kv_mine = bf16[8,128,256]{2,1,0:T(8,128)(2,1)S(1)} async-done(((bf16[8,128,256]{2,1,0:T(8,128)(2,1)}), bf16[8,128,256]{2,1,0:T(8,128)(2,1)S(1)}, u32[]{:S(2)}, u32[]{:S(2)}) %all-to-all-start) | async-done | bytes 524320 | tf_op jit(solution)/shard_map/all_to_all | solution.py:527
  30.9 2.0 %collective-permute-start.6 = (bf16[8,128,256]{2,1,0:T(8,128)(2,1)S(1)}, bf16[8,128,256]{2,1,0:T(8,128)(2,1)S(1)}, u32[]{:S(2)}, u32[]{:S(2)}) collective-permute-start(bf16[8,128,256]{2,1,0:T(8,128)(2,1)S(1)} %all-to-all-done.kv_mine), channel_id=1, source_target_pairs={{0,8},{8,0},{1,9},{9,1},{2,10},{10,2},{3,11},{11,3},{4,12},{12,4},... | collective-permute-start | bytes 1572872 | tf_op jit(solution)/shard_map/ppermute | solution.py:533
  33.1 0.4 normalize.1
  33.5 1.0 %collective-permute-done.6.kv_mate = bf16[8,128,256]{2,1,0:T(8,128)(2,1)S(1)} collective-permute-done((bf16[8,128,256]{2,1,0:T(8,128)(2,1)S(1)}, bf16[8,128,256]{2,1,0:T(8,128)(2,1)S(1)}, u32[]{:S(2)}, u32[]{:S(2)}) %collective-permute-start.6) | collective-permute-done | bytes 524320 | tf_op jit(solution)/shard_map/ppermute | solution.py:533
  34.5 3.5 %attend_forward.1 = (bf16[8,1536,256]{2,1,0:T(8,128)(2,1)S(1)}, f32[1536,128]{1,0:T(8,128)S(1)}, f32[48,128]{1,0:T(8,128)S(1)}) custom-call(s32[27]{0:T(128)S(1)} %concatenate.3.plan, bf16[1536,128]{1,0:T(8,128)(2,1)S(1)} %get-tuple-element.33.q_rows, bf16[1536,128]{1,0:T(8,128)(2,1)S(1)} %get-tuple-element.34.g_raw, ...), custom_call_target="tpu_custom_call" | custom-call | tf_op jit(solution)/shard_map/attend_forward/pallas_call | solution.py:425
  38.0 2.8 %collective-permute-start.7 = (f32[48,128]{1,0:T(8,128)S(1)}, f32[48,128]{1,0:T(8,128)S(1)}, u32[]{:S(2)}, u32[]{:S(2)}) collective-permute-start(f32[48,128]{1,0:T(8,128)S(1)} %get-tuple-element.37.stats_own), channel_id=1, source_target_pairs={{0,16},{16,0},{1,17},{17,1},{2,18},{18,2},{3,19},{19,3},{4,20},{20... | collective-permute-start | bytes 73736 | tf_op jit(solution)/shard_map/ppermute | solution.py:537
  40.8 1.4 %collective-permute-done.7.stats_mate = f32[48,128]{1,0:T(8,128)S(1)} collective-permute-done((f32[48,128]{1,0:T(8,128)S(1)}, f32[48,128]{1,0:T(8,128)S(1)}, u32[]{:S(2)}, u32[]{:S(2)}) %collective-permute-start.7) | collective-permute-done | bytes 24608 | tf_op jit(solution)/shard_map/ppermute | solution.py:537
  42.2 3.7 %attend_backward.1 = (bf16[128,768]{1,0:T(8,128)(2,1)S(1)}, bf16[128,768]{1,0:T(8,128)(2,1)S(1)}, bf16[8,1536,256]{2,1,0:T(8,128)(2,1)}, bf16[8,128,256]{2,1,0:T(8,128)(2,1)S(1)}, bf16[8,128,256]{2,1,0:T(8,128)(2,1)S(1)}) custom-call(s32[27]{0:T(128)S(1)} %concatenate.3.plan, bf16[8,1536,256]{2,1,0:T(8,128)(2,1)S(1)} %get-tuple-element.36.prob, ...), custom_call_target="tpu_custom_call" | custom-call | tf_op jit(solution)/shard_map/attend_backward/pallas_call | solution.py:451
  45.9 1.6 %collective-permute-start.9 = (bf16[8,128,256]{2,1,0:T(8,128)(2,1)S(1)}, bf16[8,128,256]{2,1,0:T(8,128)(2,1)S(1)}, u32[]{:S(2)}, u32[]{:S(2)}) collective-permute-start(bf16[8,128,256]{2,1,0:T(8,128)(2,1)S(1)} %get-tuple-element.43), channel_id=1, source_target_pairs={{0,8},{8,0},{1,9},{9,1},{2,10},{10,2},{3,11},{11,3},{4,12},{12,4},... | collective-permute-start | bytes 1572872 | tf_op jit(solution)/shard_map/ppermute | solution.py:542
  47.5 1.5 %collective-permute-done.9.other = bf16[8,128,256]{2,1,0:T(8,128)(2,1)S(1)} collective-permute-done((bf16[8,128,256]{2,1,0:T(8,128)(2,1)S(1)}, bf16[8,128,256]{2,1,0:T(8,128)(2,1)S(1)}, u32[]{:S(2)}, u32[]{:S(2)}) %collective-permute-start.9) | collective-permute-done | bytes 524320 | tf_op jit(solution)/shard_map/ppermute | solution.py:542
  49.1 0.9 %add_pair.1 = bf16[8,128,256]{2,1,0:T(8,128)(2,1)} custom-call(bf16[8,128,256]{2,1,0:T(8,128)(2,1)S(1)} %get-tuple-element.42.one, bf16[8,128,256]{2,1,0:T(8,128)(2,1)S(1)} %collective-permute-done.9.other), custom_call_target="tpu_custom_call" | custom-call | tf_op jit(solution)/shard_map/add_pair/pallas_call | solution.py:400
  50.0 4.5 %all-to-all-start.1 = ((bf16[8,128,256]{2,1,0:T(8,128)(2,1)}), bf16[8,128,256]{2,1,0:T(8,128)(2,1)S(1)}, u32[]{:S(2)}, u32[]{:S(2)}) async-start(bf16[8,128,256]{2,1,0:T(8,128)(2,1)} %add_pair.1), calls=%async_computation.1 | async-start | bytes 1048576 | tf_op jit(solution)/shard_map/all_to_all | solution.py:545
  54.5 2.7 %collective-permute-start.8 = (bf16[128,768]{1,0:T(8,128)(2,1)S(1)}, bf16[128,768]{1,0:T(8,128)(2,1)S(1)}, u32[]{:S(2)}, u32[]{:S(2)}) collective-permute-start(bf16[128,768]{1,0:T(8,128)(2,1)S(1)} %get-tuple-element.41), channel_id=1, source_target_pairs={{0,16},{16,0},{1,17},{17,1},{2,18},{18,2},{3,19},{19,3},{4,20},{20... | collective-permute-start | bytes 589832 | tf_op jit(solution)/shard_map/ppermute | solution.py:541
  57.3 2.5 %finish_mate.1 = bf16[128,768]{1,0:T(8,128)(2,1)S(1)} custom-call(s32[27]{0:T(128)S(1)} %concatenate.3.plan, bf16[8,1536,256]{2,1,0:T(8,128)(2,1)} %get-tuple-element.46.ds_in, bf16[8,128,256]{2,1,0:T(8,128)(2,1)S(1)} %all-to-all-done.kv_mine, bf16[8,128,256]{2,1,0:T(8,128)(2,1)S(1)} %collective-permute-done.6.kv_mate), custom_call_target="tpu_custom_call" | custom-call | flops 3000000000 | bytes 1024 | tf_op jit(solution)/shard_map/finish_mate/pallas_call | solution.py:476
  59.8 0.3 collective-permute-start.10
  60.1 2.5 %finish_own.1.dq_keep = bf16[128,768]{1,0:T(8,128)(2,1)S(1)} custom-call(s32[27]{0:T(128)S(1)} %concatenate.3.plan, bf16[8,1536,256]{2,1,0:T(8,128)(2,1)} %get-tuple-element.46.ds_in, bf16[8,128,256]{2,1,0:T(8,128)(2,1)S(1)} %all-to-all-done.kv_mine, bf16[8,128,256]{2,1,0:T(8,128)(2,1)S(1)} %collective-permute-done.6.kv_mate), custom_call_target="tpu_custom_call" | custom-call | flops 3000000000 | bytes 1024 | tf_op jit(solution)/shard_map/finish_own/pallas_call | solution.py:476
  62.6 4.2 %collective-permute-done.10.dq_got = bf16[128,768]{1,0:T(8,128)(2,1)S(1)} collective-permute-done((bf16[128,768]{1,0:T(8,128)(2,1)S(1)}, bf16[128,768]{1,0:T(8,128)(2,1)S(1)}, u32[]{:S(2)}, u32[]{:S(2)}) %collective-permute-start.10) | collective-permute-done | bytes 196640 | tf_op jit(solution)/shard_map/ppermute | solution.py:547
  66.8 0.8 %merge.1 = (bf16[128,768]{1,0:T(8,128)(2,1)}, bf16[128,768]{1,0:T(8,128)(2,1)}) custom-call(bf16[128,768]{1,0:T(8,128)(2,1)S(1)} %get-tuple-element.40.out_keep, bf16[128,768]{1,0:T(8,128)(2,1)S(1)} %collective-permute-done.8.out_got, bf16[128,768]{1,0:T(8,128)(2,1)S(1)} %finish_own.1.dq_keep, bf16[128,768]{1,0:T(8,128)(2,1)S(1)} %collective-permute-done.10.dq_got), custom_call_target="tpu_custom_call" | custom-call | flops 1024 | bytes 1024 | tf_op jit(solution)/shard_map/merge/pallas_call | solution.py:412
  67.6 4.8 %all-to-all-done.1 = bf16[8,128,256]{2,1,0:T(8,128)(2,1)S(1)} async-done(((bf16[8,128,256]{2,1,0:T(8,128)(2,1)}), bf16[8,128,256]{2,1,0:T(8,128)(2,1)S(1)}, u32[]{:S(2)}, u32[]{:S(2)}) %all-to-all-start.1) | async-done | bytes 524320 | tf_op jit(solution)/shard_map/all_to_all | solution.py:545
  72.6 0.6 fusion
  (24 shorter events, 0.4 us)
Async XLA Ops:
  0.6 13.9 %collective-permute-start = (bf16[128,768]{1,0:T(8,128)(2,1)}, bf16[128,768]{1,0:T(8,128)(2,1)S(1)}, u32[]{:S(2)}, u32[]{:S(2)}) collective-permute-start(bf16[128,768]{1,0:T(8,128)(2,1)} %queries.3), channel_id=1, source_target_pairs={{0,16},{16,0},{1,17},{17,1},{2,18},{18,2},{3,19},{19,3},{4,20},{20... | collective-permute-start | bytes 589832 | tf_op jit(solution)/shard_map/ppermute | solution.py:524
  4.3 17.4 %collective-permute-start.5 = (bf16[128,768]{1,0:T(8,128)(2,1)}, bf16[128,768]{1,0:T(8,128)(2,1)S(1)}, u32[]{:S(2)}, u32[]{:S(2)}) collective-permute-start(bf16[128,768]{1,0:T(8,128)(2,1)} %out_grad.1), channel_id=1, source_target_pairs={{0,16},{16,0},{1,17},{17,1},{2,18},{18,2},{3,19},{19,3},{4,20},{20... | collective-permute-start | bytes 589832 | tf_op jit(solution)/shard_map/ppermute | solution.py:525
  6.2 24.7 %all-to-all-start = ((bf16[8,128,256]{2,1,0:T(8,128)(2,1)}), bf16[8,128,256]{2,1,0:T(8,128)(2,1)S(1)}, u32[]{:S(2)}, u32[]{:S(2)}) async-start(bf16[8,128,256]{2,1,0:T(8,128)(2,1)} %get-tuple-element.27), calls=%async_computation | async-start | bytes 1048576 | tf_op jit(solution)/shard_map/all_to_all | solution.py:527
  14.5 0.7 copy-start.2
  15.2 6.4 %copy-start = (bf16[128,768]{1,0:T(8,128)(2,1)S(1)}, bf16[128,768]{1,0:T(8,128)(2,1)}, u32[]{:S(2)}) copy-start(bf16[128,768]{1,0:T(8,128)(2,1)} %queries.3) | copy-start | bytes 589828
  15.2 6.4 %copy-start.1 = (bf16[128,768]{1,0:T(8,128)(2,1)S(1)}, bf16[128,768]{1,0:T(8,128)(2,1)}, u32[]{:S(2)}) copy-start(bf16[128,768]{1,0:T(8,128)(2,1)} %out_grad.1) | copy-start | bytes 589828
  15.2 17.8 %copy-start.3 = (f32[768]{0:T(1024)S(1)}, f32[768]{0:T(1024)}, u32[]{:S(2)}) copy-start(f32[768]{0:T(1024)} %param.12) | copy-start | bytes 9220
  15.2 17.8 %copy-start.4 = (s32[8]{0:T(128)S(1)}, s32[8]{0:T(128)}, u32[]{:S(2)}) copy-start(s32[8]{0:T(128)} %param.13) | copy-start | bytes 100
  15.2 17.8 %copy-start.5 = (s32[8]{0:T(128)S(1)}, s32[8]{0:T(128)}, u32[]{:S(2)}) copy-start(s32[8]{0:T(128)} %param.14) | copy-start | bytes 100
  15.2 17.8 %copy-start.6 = (s32[8]{0:T(128)S(1)}, s32[8]{0:T(128)}, u32[]{:S(2)}) copy-start(s32[8]{0:T(128)} %param.15) | copy-start | bytes 100
  15.4 2.5 %collective-permute-start.1 = (f32[2,128]{1,0:T(2,128)S(1)}, f32[2,128]{1,0:T(2,128)S(1)}, u32[]{:S(2)}, u32[]{:S(2)}) collective-permute-start(f32[2,128]{1,0:T(2,128)S(1)} %row_squares.1), channel_id=1, source_target_pairs={{0,1},{1,0},{2,3},{3,2},{4,5},{5,4},{6,7},{7,6},{8,9},{9,8},{10,11... | collective-permute-start | bytes 3080 | tf_op jit(solution)/shard_map/ppermute | solution.py:508
  17.9 3.9 %collective-permute-start.4 = (f32[2,128]{1,0:T(2,128)S(1)}, f32[2,128]{1,0:T(2,128)S(1)}, u32[]{:S(2)}, u32[]{:S(2)}) collective-permute-start(f32[2,128]{1,0:T(2,128)S(1)} %add.12), channel_id=1, source_target_pairs={{0,6},{2,0},{4,2},{6,4},{1,7},{3,1},{5,3},{7,5},{8,14},{10,8},{12,... | collective-permute-start | bytes 3080 | tf_op jit(solution)/shard_map/ppermute | solution.py:510
  20.6 4.2 %collective-permute-start.3 = (f32[2,128]{1,0:T(2,128)S(1)}, f32[2,128]{1,0:T(2,128)S(1)}, u32[]{:S(2)}, u32[]{:S(2)}) collective-permute-start(f32[2,128]{1,0:T(2,128)S(1)} %add.12), channel_id=1, source_target_pairs={{0,4},{2,6},{4,0},{6,2},{1,5},{3,7},{5,1},{7,3},{8,12},{10,14},{12... | collective-permute-start | bytes 3080 | tf_op jit(solution)/shard_map/ppermute | solution.py:510
  20.9 3.9 %collective-permute-start.2 = (f32[2,128]{1,0:T(2,128)S(1)}, f32[2,128]{1,0:T(2,128)S(1)}, u32[]{:S(2)}, u32[]{:S(2)}) collective-permute-start(f32[2,128]{1,0:T(2,128)S(1)} %add.12), channel_id=1, source_target_pairs={{0,2},{2,4},{4,6},{6,0},{1,3},{3,5},{5,7},{7,1},{8,10},{10,12},{12... | collective-permute-start | bytes 3080 | tf_op jit(solution)/shard_map/ppermute | solution.py:510
  30.9 3.6 %collective-permute-start.6 = (bf16[8,128,256]{2,1,0:T(8,128)(2,1)S(1)}, bf16[8,128,256]{2,1,0:T(8,128)(2,1)S(1)}, u32[]{:S(2)}, u32[]{:S(2)}) collective-permute-start(bf16[8,128,256]{2,1,0:T(8,128)(2,1)S(1)} %all-to-all-done.kv_mine), channel_id=1, source_target_pairs={{0,8},{8,0},{1,9},{9,1},{2,10},{10,2},{3,11},{11,3},{4,12},{12,4},... | collective-permute-start | bytes 1572872 | tf_op jit(solution)/shard_map/ppermute | solution.py:533
  38.0 4.2 %collective-permute-start.7 = (f32[48,128]{1,0:T(8,128)S(1)}, f32[48,128]{1,0:T(8,128)S(1)}, u32[]{:S(2)}, u32[]{:S(2)}) collective-permute-start(f32[48,128]{1,0:T(8,128)S(1)} %get-tuple-element.37.stats_own), channel_id=1, source_target_pairs={{0,16},{16,0},{1,17},{17,1},{2,18},{18,2},{3,19},{19,3},{4,20},{20... | collective-permute-start | bytes 73736 | tf_op jit(solution)/shard_map/ppermute | solution.py:537
  45.9 3.1 %collective-permute-start.9 = (bf16[8,128,256]{2,1,0:T(8,128)(2,1)S(1)}, bf16[8,128,256]{2,1,0:T(8,128)(2,1)S(1)}, u32[]{:S(2)}, u32[]{:S(2)}) collective-permute-start(bf16[8,128,256]{2,1,0:T(8,128)(2,1)S(1)} %get-tuple-element.43), channel_id=1, source_target_pairs={{0,8},{8,0},{1,9},{9,1},{2,10},{10,2},{3,11},{11,3},{4,12},{12,4},... | collective-permute-start | bytes 1572872 | tf_op jit(solution)/shard_map/ppermute | solution.py:542
  50.0 22.5 %all-to-all-start.1 = ((bf16[8,128,256]{2,1,0:T(8,128)(2,1)}), bf16[8,128,256]{2,1,0:T(8,128)(2,1)S(1)}, u32[]{:S(2)}, u32[]{:S(2)}) async-start(bf16[8,128,256]{2,1,0:T(8,128)(2,1)} %add_pair.1), calls=%async_computation.1 | async-start | bytes 1048576 | tf_op jit(solution)/shard_map/all_to_all | solution.py:545
  54.5 8.1 %collective-permute-start.8 = (bf16[128,768]{1,0:T(8,128)(2,1)S(1)}, bf16[128,768]{1,0:T(8,128)(2,1)S(1)}, u32[]{:S(2)}, u32[]{:S(2)}) collective-permute-start(bf16[128,768]{1,0:T(8,128)(2,1)S(1)} %get-tuple-element.41), channel_id=1, source_target_pairs={{0,16},{16,0},{1,17},{17,1},{2,18},{18,2},{3,19},{19,3},{4,20},{20... | collective-permute-start | bytes 589832 | tf_op jit(solution)/shard_map/ppermute | solution.py:541
  59.8 7.1 %collective-permute-start.10 = (bf16[128,768]{1,0:T(8,128)(2,1)S(1)}, bf16[128,768]{1,0:T(8,128)(2,1)S(1)}, u32[]{:S(2)}, u32[]{:S(2)}) collective-permute-start(bf16[128,768]{1,0:T(8,128)(2,1)S(1)} %finish_mate.1), channel_id=1, source_target_pairs={{0,16},{16,0},{1,17},{17,1},{2,18},{18,2},{3,19},{19,3},{4,20},{20... | collective-permute-start | bytes 589832 | tf_op jit(solution)/shard_map/ppermute | solution.py:547

commit v3 on v2

--- a/solution.py
+++ b/solution.py
@@ -143,32 +143,26 @@
     half = heads * tok
     keys_n = 2 * tok
     count, own_span = visible_slots(plan, order, spans)
-    row_max[...] = jnp.full_like(row_max, NEG)
-    row_sum[...] = jnp.zeros_like(row_sum)
-    acc[...] = jnp.zeros_like(acc)
     chunks = [slice(r, r + group) for r in range(0, 2 * half, group)]
 
-    def score_block(i, masked):
-        slot = order[i]
-        keys = jnp.concatenate([kv_mine[slot, :, :dim], kv_mate[slot, :, :dim]], axis=0)
-        if masked:
-            free = plan[3 + own_span] == 0
-            q_t = lax.broadcasted_iota(jnp.int32, (group, keys_n), 0) % tok
-            k_t = lax.broadcasted_iota(jnp.int32, (group, keys_n), 1)
-            core = plan[2]
-            k_pos = plan[1] * keys_n + jnp.where(
-                k_t < tok, core * tok + k_t, (1 - core) * tok + k_t - tok
-            )
+    def score_own():
+        keys = stacked(order, 0, 1, slice(0, dim), kv_mine, kv_mate)
+        free = plan[3 + own_span] == 0
+        q_t = lax.broadcasted_iota(jnp.int32, (group, keys_n), 0) % tok
+        k_t = lax.broadcasted_iota(jnp.int32, (group, keys_n), 1)
+        core = plan[2]
+        k_pos = plan[1] * keys_n + jnp.where(
+            k_t < tok, core * tok + k_t, (1 - core) * tok + k_t - tok
+        )
         for c in chunks:
+            q_xh = plan[1] if c.start < half else 1 - plan[1]
+            q_pos = (q_xh * 2 + core) * tok + q_t
             s = dot_rows(q_rows[c, :], keys)
-            if masked:
-                q_xh = plan[1] if c.start < half else 1 - plan[1]
-                q_pos = (q_xh * 2 + core) * tok + q_t
-                s = jnp.where((k_pos <= q_pos) | free, s, NEG)
-            score[i, c, :] = s
-            row_max[c, :] = functools.reduce(jnp.maximum, lane_tiles(s), row_max[c, :])
-
-    score_block(0, True)
+            s = jnp.where((k_pos <= q_pos) | free, s, NEG)
+            score[0, c, :] = s
+            row_max[c, :] = functools.reduce(jnp.maximum, lane_tiles(s))
+
+    score_own()
 
     def score_blocks(first, n):
         keys = stacked(order, first, n, slice(0, dim), kv_mine, kv_mate)
@@ -184,19 +178,33 @@
         top = jnp.max(row_max[c, :], axis=1, keepdims=True)
         row_max[c, :] = jnp.broadcast_to(top, (group, LANES))
 
-    def weigh(first, n):
+    def weigh(first, n, start):
         values = stacked(order, first, n, slice(dim, 2 * dim), kv_mine, kv_mate)
         for c in chunks:
             top = row_max[c, :]
             blocks = [lane_tiles(score[first + k, c, :]) for k in range(n)]
             tiles = [[jnp.exp2(t - top) for t in b] for b in blocks]
-            row_sum[c, :] += functools.reduce(jnp.add, sum(tiles, []))
+            sums = functools.reduce(jnp.add, sum(tiles, []))
+            row_sum[c, :] = sums if start else row_sum[c, :] + sums
             p = [jnp.concatenate(b, axis=1).astype(jnp.bfloat16) for b in tiles]
             for k in range(n):
                 prob[first + k, c, :] = p[k]
-            acc[c, :] += dot(jnp.concatenate(p, axis=1), values)
-
-    by_pairs(count, weigh)
+            mixed = dot(jnp.concatenate(p, axis=1), values)
+            acc[c, :] = mixed if start else acc[c, :] + mixed
+
+    odd = count % 2
+
+    @pl.when(odd == 1)
+    def _():
+        weigh(0, 1, True)
+
+    @pl.when(odd == 0)
+    def _():
+        weigh(0, 2, True)
+
+    @pl.loop(0, (count - 1) // 2)
+    def _(i):
+        weigh(2 * i + 2 - odd, 2, False)
 
     lane = lax.broadcasted_iota(jnp.int32, (tok, LANES), 1)
     table = jnp.zeros((tok, LANES), jnp.float32)
@@ -324,10 +332,21 @@
         d_queries[:, h * dim : (h + 1) * dim] = rows_of.astype(jnp.bfloat16)
 
 
-def spread(keys, values, queries, out, squares):
+def spread(keys_in, values_in, queries_in, out, squares, keys, values, queries, sems):
+    moved = [
+        pltpu.make_async_copy(source, target, sems.at[n])
+        for n, (source, target) in enumerate(
+            ((keys_in, keys), (values_in, values), (queries_in, queries))
+        )
+    ]
+    for copy in moved:
+        copy.start()
+    moved[0].wait()
+    moved[1].wait()
     both = jnp.concatenate([keys[...], values[...]], axis=1)
     for n in range(out.shape[0]):
         out[n] = both
+    moved[2].wait()
     squares[...] = squares_of(queries[...])
 
 
@@ -492,16 +511,20 @@
 
 def spread_call(keys, values, queries, n_z):
     tok, dim = keys.shape
+    arrays = [pltpu.with_memory_space_constraint(x, pltpu.HBM) for x in (keys, values, queries)]
     return pl.pallas_call(
         spread,
         out_shape=(
             jax.ShapeDtypeStruct((n_z, tok, 2 * dim), jnp.bfloat16),
             jax.ShapeDtypeStruct((1, tok), jnp.float32),
         ),
-        in_specs=[VMEM_SPEC] * 3,
+        in_specs=[HBM_SPEC] * 3,
         out_specs=(VMEM_SPEC,) * 2,
+        scratch_shapes=[pltpu.VMEM(x.shape, x.dtype) for x in (keys, values, queries)]
+        + [pltpu.SemaphoreType.DMA((3,))],
+        compiler_params=small_params(),
         name="spread",
-    )(keys, values, queries)
+    )(*arrays)
 
 
 def head_sum(x):

time: 73.5 us -> 73.8 us (level)
  no operation moved by 1% of the time
where the time goes in v3:
time: 73.8 us; the launch traced here: 73.5 us
  starting transfers between devices  31.5 us (43%)
  waiting for transfers between devices  24 us (33%)
  Pallas kernels  16.3 us (22%)
  between operations  0.78 us (1%)
  local copies, waits for them, and re-layouts  0.75 us (1%)
    all_to_all x1, starting transfers between devices, shards(): kv_mine = lax.all_to_all(kv_out, 'z', 0, 0)  8.32 us
    all_to_all x1, waiting for transfers between devices, shards(): kv_mine = lax.all_to_all(kv_out, 'z', 0, 0)  6.69 us
    pallas_call x2, Pallas kernels, finish_call(): pl.pallas_call(functools.partial(finish, tok=tok, heads=heads, dim=dim, f...  5.03 us
    all_to_all x1, waiting for transfers between devices, shards(): pieces = lax.all_to_all(chip, 'z', 0, 0)  4.84 us
    all_to_all x1, starting transfers between devices, shards(): pieces = lax.all_to_all(chip, 'z', 0, 0)  4.83 us
    ppermute x1, waiting for transfers between devices, shards(): dq_got = lax.ppermute(dq_give, 'xh', SWAP)  4.22 us
    ppermute x3, starting transfers between devices, head_sum(): lax.ppermute(x, 'y', [(i, (i + d) % n) for i in range(n)])  3.77 us
    pallas_call x1, Pallas kernels, backward_call(): pl.pallas_call(functools.partial(backward, tok=tok, heads=heads, dim=dim,...  3.71 us
  transfers between devices with their start and end apart: 13, of which 9 were waited for; matrix products, arithmetic and copies ran while one was open for 0% of the time, Pallas kernels for 11%

profile of v3, /device:TPU:1, one launch (start us, length us, event | category | flops | bytes accessed | tf_op | source)
XLA Modules:
  0.0 73.5 jit_solution(7477634407442158003)
XLA Ops:
  0.6 3.7 %collective-permute-start = (bf16[128,768]{1,0:T(8,128)(2,1)}, bf16[128,768]{1,0:T(8,128)(2,1)S(1)}, u32[]{:S(2)}, u32[]{:S(2)}) collective-permute-start(bf16[128,768]{1,0:T(8,128)(2,1)} %queries.1), channel_id=1, source_target_pairs={{0,16},{16,0},{1,17},{17,1},{2,18},{18,2},{3,19},{19,3},{4,20},{20... | collective-permute-start | bytes 589832 | tf_op jit(solution)/shard_map/ppermute | solution.py:547
  4.3 0.1 collective-permute-start.5
  4.4 1.8 %spread.1 = (bf16[8,128,256]{2,1,0:T(8,128)(2,1)}, f32[1,128]{1,0:T(1,128)S(1)}) custom-call(bf16[128,128]{1,0:T(8,128)(2,1)} %keys_in.1, bf16[128,128]{1,0:T(8,128)(2,1)} %values_in.1, bf16[128,768]{1,0:T(8,128)(2,1)} %queries.1), custom_call_target="tpu_custom_call" | custom-call | tf_op jit(solution)/shard_map/spread/pallas_call | solution.py:515
  6.2 8.3 %all-to-all-start = ((bf16[8,128,256]{2,1,0:T(8,128)(2,1)}), bf16[8,128,256]{2,1,0:T(8,128)(2,1)S(1)}, u32[]{:S(2)}, u32[]{:S(2)}) async-start(bf16[8,128,256]{2,1,0:T(8,128)(2,1)} %get-tuple-element.27), calls=%async_computation | async-start | bytes 1048576 | tf_op jit(solution)/shard_map/all_to_all | solution.py:550
  14.6 0.1 row_squares.1
  14.7 1.3 %collective-permute-start.1 = (f32[2,128]{1,0:T(2,128)S(1)}, f32[2,128]{1,0:T(2,128)S(1)}, u32[]{:S(2)}, u32[]{:S(2)}) collective-permute-start(f32[2,128]{1,0:T(2,128)S(1)} %row_squares.1), channel_id=1, source_target_pairs={{0,1},{1,0},{2,3},{3,2},{4,5},{5,4},{6,7},{7,6},{8,9},{9,8},{10,11... | collective-permute-start | bytes 3080 | tf_op jit(solution)/shard_map/ppermute | solution.py:531
  16.0 1.2 %collective-permute-done.1 = f32[2,128]{1,0:T(2,128)S(1)} collective-permute-done((f32[2,128]{1,0:T(2,128)S(1)}, f32[2,128]{1,0:T(2,128)S(1)}, u32[]{:S(2)}, u32[]{:S(2)}) %collective-permute-start.1) | collective-permute-done | bytes 1056 | tf_op jit(solution)/shard_map/ppermute | solution.py:531
  17.2 2.7 %collective-permute-start.4 = (f32[2,128]{1,0:T(2,128)S(1)}, f32[2,128]{1,0:T(2,128)S(1)}, u32[]{:S(2)}, u32[]{:S(2)}) collective-permute-start(f32[2,128]{1,0:T(2,128)S(1)} %add.12), channel_id=1, source_target_pairs={{0,6},{2,0},{4,2},{6,4},{1,7},{3,1},{5,3},{7,5},{8,14},{10,8},{12,... | collective-permute-start | bytes 3080 | tf_op jit(solution)/shard_map/ppermute | solution.py:533
  20.0 0.3 collective-permute-start.3
  20.3 0.7 collective-permute-start.2
  21.0 0.1 prepare.1
  21.2 3.0 %collective-permute-done.3 = f32[2,128]{1,0:T(2,128)S(1)} collective-permute-done((f32[2,128]{1,0:T(2,128)S(1)}, f32[2,128]{1,0:T(2,128)S(1)}, u32[]{:S(2)}, u32[]{:S(2)}) %collective-permute-start.3) | collective-permute-done | bytes 1056 | tf_op jit(solution)/shard_map/ppermute | solution.py:533
  24.2 6.7 %all-to-all-done.kv_mine = bf16[8,128,256]{2,1,0:T(8,128)(2,1)S(1)} async-done(((bf16[8,128,256]{2,1,0:T(8,128)(2,1)}), bf16[8,128,256]{2,1,0:T(8,128)(2,1)S(1)}, u32[]{:S(2)}, u32[]{:S(2)}) %all-to-all-start) | async-done | bytes 524320 | tf_op jit(solution)/shard_map/all_to_all | solution.py:550
  30.9 2.0 %collective-permute-start.6 = (bf16[8,128,256]{2,1,0:T(8,128)(2,1)S(1)}, bf16[8,128,256]{2,1,0:T(8,128)(2,1)S(1)}, u32[]{:S(2)}, u32[]{:S(2)}) collective-permute-start(bf16[8,128,256]{2,1,0:T(8,128)(2,1)S(1)} %all-to-all-done.kv_mine), channel_id=1, source_target_pairs={{0,8},{8,0},{1,9},{9,1},{2,10},{10,2},{3,11},{11,3},{4,12},{12,4},... | collective-permute-start | bytes 1572872 | tf_op jit(solution)/shard_map/ppermute | solution.py:556
  33.1 0.4 normalize.1
  33.5 1.0 %collective-permute-done.6.kv_mate = bf16[8,128,256]{2,1,0:T(8,128)(2,1)S(1)} collective-permute-done((bf16[8,128,256]{2,1,0:T(8,128)(2,1)S(1)}, bf16[8,128,256]{2,1,0:T(8,128)(2,1)S(1)}, u32[]{:S(2)}, u32[]{:S(2)}) %collective-permute-start.6) | collective-permute-done | bytes 524320 | tf_op jit(solution)/shard_map/ppermute | solution.py:556
  34.5 3.5 %attend_forward.1 = (bf16[8,1536,256]{2,1,0:T(8,128)(2,1)S(1)}, f32[1536,128]{1,0:T(8,128)S(1)}, f32[48,128]{1,0:T(8,128)S(1)}) custom-call(s32[27]{0:T(128)S(1)} %concatenate.3.plan, bf16[1536,128]{1,0:T(8,128)(2,1)S(1)} %get-tuple-element.33.q_rows, bf16[1536,128]{1,0:T(8,128)(2,1)S(1)} %get-tuple-element.34.g_raw, ...), custom_call_target="tpu_custom_call" | custom-call | tf_op jit(solution)/shard_map/attend_forward/pallas_call | solution.py:444
  38.0 2.8 %collective-permute-start.7 = (f32[48,128]{1,0:T(8,128)S(1)}, f32[48,128]{1,0:T(8,128)S(1)}, u32[]{:S(2)}, u32[]{:S(2)}) collective-permute-start(f32[48,128]{1,0:T(8,128)S(1)} %get-tuple-element.37.stats_own), channel_id=1, source_target_pairs={{0,16},{16,0},{1,17},{17,1},{2,18},{18,2},{3,19},{19,3},{4,20},{20... | collective-permute-start | bytes 73736 | tf_op jit(solution)/shard_map/ppermute | solution.py:560
  40.8 1.4 %collective-permute-done.7.stats_mate = f32[48,128]{1,0:T(8,128)S(1)} collective-permute-done((f32[48,128]{1,0:T(8,128)S(1)}, f32[48,128]{1,0:T(8,128)S(1)}, u32[]{:S(2)}, u32[]{:S(2)}) %collective-permute-start.7) | collective-permute-done | bytes 24608 | tf_op jit(solution)/shard_map/ppermute | solution.py:560
  42.2 3.7 %attend_backward.1 = (bf16[128,768]{1,0:T(8,128)(2,1)S(1)}, bf16[128,768]{1,0:T(8,128)(2,1)S(1)}, bf16[8,1536,256]{2,1,0:T(8,128)(2,1)}, bf16[8,128,256]{2,1,0:T(8,128)(2,1)S(1)}, bf16[8,128,256]{2,1,0:T(8,128)(2,1)S(1)}) custom-call(s32[27]{0:T(128)S(1)} %concatenate.3.plan, bf16[8,1536,256]{2,1,0:T(8,128)(2,1)S(1)} %get-tuple-element.36.prob, ...), custom_call_target="tpu_custom_call" | custom-call | tf_op jit(solution)/shard_map/attend_backward/pallas_call | solution.py:470
  45.9 1.6 %collective-permute-start.9 = (bf16[8,128,256]{2,1,0:T(8,128)(2,1)S(1)}, bf16[8,128,256]{2,1,0:T(8,128)(2,1)S(1)}, u32[]{:S(2)}, u32[]{:S(2)}) collective-permute-start(bf16[8,128,256]{2,1,0:T(8,128)(2,1)S(1)} %get-tuple-element.43), channel_id=1, source_target_pairs={{0,8},{8,0},{1,9},{9,1},{2,10},{10,2},{3,11},{11,3},{4,12},{12,4},... | collective-permute-start | bytes 1572872 | tf_op jit(solution)/shard_map/ppermute | solution.py:565
  47.5 1.5 %collective-permute-done.9.other = bf16[8,128,256]{2,1,0:T(8,128)(2,1)S(1)} collective-permute-done((bf16[8,128,256]{2,1,0:T(8,128)(2,1)S(1)}, bf16[8,128,256]{2,1,0:T(8,128)(2,1)S(1)}, u32[]{:S(2)}, u32[]{:S(2)}) %collective-permute-start.9) | collective-permute-done | bytes 524320 | tf_op jit(solution)/shard_map/ppermute | solution.py:565
  49.1 0.9 %add_pair.1 = bf16[8,128,256]{2,1,0:T(8,128)(2,1)} custom-call(bf16[8,128,256]{2,1,0:T(8,128)(2,1)S(1)} %get-tuple-element.42.one, bf16[8,128,256]{2,1,0:T(8,128)(2,1)S(1)} %collective-permute-done.9.other), custom_call_target="tpu_custom_call" | custom-call | tf_op jit(solution)/shard_map/add_pair/pallas_call | solution.py:419
  50.0 4.8 %all-to-all-start.1 = ((bf16[8,128,256]{2,1,0:T(8,128)(2,1)}), bf16[8,128,256]{2,1,0:T(8,128)(2,1)S(1)}, u32[]{:S(2)}, u32[]{:S(2)}) async-start(bf16[8,128,256]{2,1,0:T(8,128)(2,1)} %add_pair.1), calls=%async_computation.1 | async-start | bytes 1048576 | tf_op jit(solution)/shard_map/all_to_all | solution.py:568
  54.8 2.7 %collective-permute-start.8 = (bf16[128,768]{1,0:T(8,128)(2,1)S(1)}, bf16[128,768]{1,0:T(8,128)(2,1)S(1)}, u32[]{:S(2)}, u32[]{:S(2)}) collective-permute-start(bf16[128,768]{1,0:T(8,128)(2,1)S(1)} %get-tuple-element.41), channel_id=1, source_target_pairs={{0,16},{16,0},{1,17},{17,1},{2,18},{18,2},{3,19},{19,3},{4,20},{20... | collective-permute-start | bytes 589832 | tf_op jit(solution)/shard_map/ppermute | solution.py:564
  57.6 2.5 %finish_mate.1 = bf16[128,768]{1,0:T(8,128)(2,1)S(1)} custom-call(s32[27]{0:T(128)S(1)} %concatenate.3.plan, bf16[8,1536,256]{2,1,0:T(8,128)(2,1)} %get-tuple-element.46.ds_in, bf16[8,128,256]{2,1,0:T(8,128)(2,1)S(1)} %all-to-all-done.kv_mine, bf16[8,128,256]{2,1,0:T(8,128)(2,1)S(1)} %collective-permute-done.6.kv_mate), custom_call_target="tpu_custom_call" | custom-call | flops 3000000000 | bytes 1024 | tf_op jit(solution)/shard_map/finish_mate/pallas_call | solution.py:495
  60.1 0.3 collective-permute-start.10
  60.4 2.5 %finish_own.1.dq_keep = bf16[128,768]{1,0:T(8,128)(2,1)S(1)} custom-call(s32[27]{0:T(128)S(1)} %concatenate.3.plan, bf16[8,1536,256]{2,1,0:T(8,128)(2,1)} %get-tuple-element.46.ds_in, bf16[8,128,256]{2,1,0:T(8,128)(2,1)S(1)} %all-to-all-done.kv_mine, bf16[8,128,256]{2,1,0:T(8,128)(2,1)S(1)} %collective-permute-done.6.kv_mate), custom_call_target="tpu_custom_call" | custom-call | flops 3000000000 | bytes 1024 | tf_op jit(solution)/shard_map/finish_own/pallas_call | solution.py:495
  62.9 4.2 %collective-permute-done.10.dq_got = bf16[128,768]{1,0:T(8,128)(2,1)S(1)} collective-permute-done((bf16[128,768]{1,0:T(8,128)(2,1)S(1)}, bf16[128,768]{1,0:T(8,128)(2,1)S(1)}, u32[]{:S(2)}, u32[]{:S(2)}) %collective-permute-start.10) | collective-permute-done | bytes 196640 | tf_op jit(solution)/shard_map/ppermute | solution.py:570
  67.1 0.8 %merge.1 = (bf16[128,768]{1,0:T(8,128)(2,1)}, bf16[128,768]{1,0:T(8,128)(2,1)}) custom-call(bf16[128,768]{1,0:T(8,128)(2,1)S(1)} %get-tuple-element.40.out_keep, bf16[128,768]{1,0:T(8,128)(2,1)S(1)} %collective-permute-done.8.out_got, bf16[128,768]{1,0:T(8,128)(2,1)S(1)} %finish_own.1.dq_keep, bf16[128,768]{1,0:T(8,128)(2,1)S(1)} %collective-permute-done.10.dq_got), custom_call_target="tpu_custom_call" | custom-call | flops 1024 | bytes 1024 | tf_op jit(solution)/shard_map/merge/pallas_call | solution.py:431
  67.9 4.8 %all-to-all-done.1 = bf16[8,128,256]{2,1,0:T(8,128)(2,1)S(1)} async-done(((bf16[8,128,256]{2,1,0:T(8,128)(2,1)}), bf16[8,128,256]{2,1,0:T(8,128)(2,1)S(1)}, u32[]{:S(2)}, u32[]{:S(2)}) %all-to-all-start.1) | async-done | bytes 524320 | tf_op jit(solution)/shard_map/all_to_all | solution.py:568
  72.9 0.6 fusion
  (22 shorter events, 0.3 us)
Async XLA Ops:
  0.6 13.9 %collective-permute-start = (bf16[128,768]{1,0:T(8,128)(2,1)}, bf16[128,768]{1,0:T(8,128)(2,1)S(1)}, u32[]{:S(2)}, u32[]{:S(2)}) collective-permute-start(bf16[128,768]{1,0:T(8,128)(2,1)} %queries.1), channel_id=1, source_target_pairs={{0,16},{16,0},{1,17},{17,1},{2,18},{18,2},{3,19},{19,3},{4,20},{20... | collective-permute-start | bytes 589832 | tf_op jit(solution)/shard_map/ppermute | solution.py:547
  4.3 16.7 %collective-permute-start.5 = (bf16[128,768]{1,0:T(8,128)(2,1)}, bf16[128,768]{1,0:T(8,128)(2,1)S(1)}, u32[]{:S(2)}, u32[]{:S(2)}) collective-permute-start(bf16[128,768]{1,0:T(8,128)(2,1)} %out_grad.1), channel_id=1, source_target_pairs={{0,16},{16,0},{1,17},{17,1},{2,18},{18,2},{3,19},{19,3},{4,20},{20... | collective-permute-start | bytes 589832 | tf_op jit(solution)/shard_map/ppermute | solution.py:548
  6.2 24.7 %all-to-all-start = ((bf16[8,128,256]{2,1,0:T(8,128)(2,1)}), bf16[8,128,256]{2,1,0:T(8,128)(2,1)S(1)}, u32[]{:S(2)}, u32[]{:S(2)}) async-start(bf16[8,128,256]{2,1,0:T(8,128)(2,1)} %get-tuple-element.27), calls=%async_computation | async-start | bytes 1048576 | tf_op jit(solution)/shard_map/all_to_all | solution.py:550
  14.5 6.5 %copy-start = (bf16[128,768]{1,0:T(8,128)(2,1)S(1)}, bf16[128,768]{1,0:T(8,128)(2,1)}, u32[]{:S(2)}) copy-start(bf16[128,768]{1,0:T(8,128)(2,1)} %queries.1) | copy-start | bytes 589828
  14.5 6.5 %copy-start.1 = (bf16[128,768]{1,0:T(8,128)(2,1)S(1)}, bf16[128,768]{1,0:T(8,128)(2,1)}, u32[]{:S(2)}) copy-start(bf16[128,768]{1,0:T(8,128)(2,1)} %out_grad.1) | copy-start | bytes 589828
  14.5 18.4 %copy-start.2 = (f32[768]{0:T(1024)S(1)}, f32[768]{0:T(1024)}, u32[]{:S(2)}) copy-start(f32[768]{0:T(1024)} %param.12) | copy-start | bytes 9220
  14.6 18.4 %copy-start.3 = (s32[8]{0:T(128)S(1)}, s32[8]{0:T(128)}, u32[]{:S(2)}) copy-start(s32[8]{0:T(128)} %param.13) | copy-start | bytes 100
  14.6 18.4 %copy-start.4 = (s32[8]{0:T(128)S(1)}, s32[8]{0:T(128)}, u32[]{:S(2)}) copy-start(s32[8]{0:T(128)} %param.14) | copy-start | bytes 100
  14.6 18.4 %copy-start.5 = (s32[8]{0:T(128)S(1)}, s32[8]{0:T(128)}, u32[]{:S(2)}) copy-start(s32[8]{0:T(128)} %param.15) | copy-start | bytes 100
  14.7 2.5 %collective-permute-start.1 = (f32[2,128]{1,0:T(2,128)S(1)}, f32[2,128]{1,0:T(2,128)S(1)}, u32[]{:S(2)}, u32[]{:S(2)}) collective-permute-start(f32[2,128]{1,0:T(2,128)S(1)} %row_squares.1), channel_id=1, source_target_pairs={{0,1},{1,0},{2,3},{3,2},{4,5},{5,4},{6,7},{7,6},{8,9},{9,8},{10,11... | collective-permute-start | bytes 3080 | tf_op jit(solution)/shard_map/ppermute | solution.py:531
  17.2 3.9 %collective-permute-start.4 = (f32[2,128]{1,0:T(2,128)S(1)}, f32[2,128]{1,0:T(2,128)S(1)}, u32[]{:S(2)}, u32[]{:S(2)}) collective-permute-start(f32[2,128]{1,0:T(2,128)S(1)} %add.12), channel_id=1, source_target_pairs={{0,6},{2,0},{4,2},{6,4},{1,7},{3,1},{5,3},{7,5},{8,14},{10,8},{12,... | collective-permute-start | bytes 3080 | tf_op jit(solution)/shard_map/ppermute | solution.py:533
  20.0 4.2 %collective-permute-start.3 = (f32[2,128]{1,0:T(2,128)S(1)}, f32[2,128]{1,0:T(2,128)S(1)}, u32[]{:S(2)}, u32[]{:S(2)}) collective-permute-start(f32[2,128]{1,0:T(2,128)S(1)} %add.12), channel_id=1, source_target_pairs={{0,4},{2,6},{4,0},{6,2},{1,5},{3,7},{5,1},{7,3},{8,12},{10,14},{12... | collective-permute-start | bytes 3080 | tf_op jit(solution)/shard_map/ppermute | solution.py:533
  20.3 3.9 %collective-permute-start.2 = (f32[2,128]{1,0:T(2,128)S(1)}, f32[2,128]{1,0:T(2,128)S(1)}, u32[]{:S(2)}, u32[]{:S(2)}) collective-permute-start(f32[2,128]{1,0:T(2,128)S(1)} %add.12), channel_id=1, source_target_pairs={{0,2},{2,4},{4,6},{6,0},{1,3},{3,5},{5,7},{7,1},{8,10},{10,12},{12... | collective-permute-start | bytes 3080 | tf_op jit(solution)/shard_map/ppermute | solution.py:533
  30.9 3.6 %collective-permute-start.6 = (bf16[8,128,256]{2,1,0:T(8,128)(2,1)S(1)}, bf16[8,128,256]{2,1,0:T(8,128)(2,1)S(1)}, u32[]{:S(2)}, u32[]{:S(2)}) collective-permute-start(bf16[8,128,256]{2,1,0:T(8,128)(2,1)S(1)} %all-to-all-done.kv_mine), channel_id=1, source_target_pairs={{0,8},{8,0},{1,9},{9,1},{2,10},{10,2},{3,11},{11,3},{4,12},{12,4},... | collective-permute-start | bytes 1572872 | tf_op jit(solution)/shard_map/ppermute | solution.py:556
  38.0 4.2 %collective-permute-start.7 = (f32[48,128]{1,0:T(8,128)S(1)}, f32[48,128]{1,0:T(8,128)S(1)}, u32[]{:S(2)}, u32[]{:S(2)}) collective-permute-start(f32[48,128]{1,0:T(8,128)S(1)} %get-tuple-element.37.stats_own), channel_id=1, source_target_pairs={{0,16},{16,0},{1,17},{17,1},{2,18},{18,2},{3,19},{19,3},{4,20},{20... | collective-permute-start | bytes 73736 | tf_op jit(solution)/shard_map/ppermute | solution.py:560
  45.9 3.1 %collective-permute-start.9 = (bf16[8,128,256]{2,1,0:T(8,128)(2,1)S(1)}, bf16[8,128,256]{2,1,0:T(8,128)(2,1)S(1)}, u32[]{:S(2)}, u32[]{:S(2)}) collective-permute-start(bf16[8,128,256]{2,1,0:T(8,128)(2,1)S(1)} %get-tuple-element.43), channel_id=1, source_target_pairs={{0,8},{8,0},{1,9},{9,1},{2,10},{10,2},{3,11},{11,3},{4,12},{12,4},... | collective-permute-start | bytes 1572872 | tf_op jit(solution)/shard_map/ppermute | solution.py:565
  50.0 22.8 %all-to-all-start.1 = ((bf16[8,128,256]{2,1,0:T(8,128)(2,1)}), bf16[8,128,256]{2,1,0:T(8,128)(2,1)S(1)}, u32[]{:S(2)}, u32[]{:S(2)}) async-start(bf16[8,128,256]{2,1,0:T(8,128)(2,1)} %add_pair.1), calls=%async_computation.1 | async-start | bytes 1048576 | tf_op jit(solution)/shard_map/all_to_all | solution.py:568
  54.8 8.1 %collective-permute-start.8 = (bf16[128,768]{1,0:T(8,128)(2,1)S(1)}, bf16[128,768]{1,0:T(8,128)(2,1)S(1)}, u32[]{:S(2)}, u32[]{:S(2)}) collective-permute-start(bf16[128,768]{1,0:T(8,128)(2,1)S(1)} %get-tuple-element.41), channel_id=1, source_target_pairs={{0,16},{16,0},{1,17},{17,1},{2,18},{18,2},{3,19},{19,3},{4,20},{20... | collective-permute-start | bytes 589832 | tf_op jit(solution)/shard_map/ppermute | solution.py:564
  60.1 7.1 %collective-permute-start.10 = (bf16[128,768]{1,0:T(8,128)(2,1)S(1)}, bf16[128,768]{1,0:T(8,128)(2,1)S(1)}, u32[]{:S(2)}, u32[]{:S(2)}) collective-permute-start(bf16[128,768]{1,0:T(8,128)(2,1)S(1)} %finish_mate.1), channel_id=1, source_target_pairs={{0,16},{16,0},{1,17},{17,1},{2,18},{18,2},{3,19},{19,3},{4,20},{20... | collective-permute-start | bytes 589832 | tf_op jit(solution)/shard_map/ppermute | solution.py:570

commit v4 on v2

--- a/solution.py
+++ b/solution.py
@@ -120,12 +120,14 @@
             q_cols[:, r] = jnp.transpose(normed)
 
 
-def prepare(queries, q_mate, out_grad, g_mate, q_raw, g_raw, *, tok, heads, dim):
+def prepare(queries, q_mate, out_grad, g_mate, q_raw, g_raw, g_turned, *, tok, heads, dim):
     for side, (q_part, g_part) in enumerate(((queries, out_grad), (q_mate, g_mate))):
         for h in range(heads):
             first = (side * heads + h) * tok
             q_raw[first : first + tok, :] = q_part[:, h * dim : (h + 1) * dim]
-            g_raw[first : first + tok, :] = g_part[:, h * dim : (h + 1) * dim]
+            g_head = g_part[:, h * dim : (h + 1) * dim]
+            g_raw[first : first + tok, :] = g_head
+            g_turned[:, first : first + tok] = jnp.transpose(g_head)
 
 
 def merge(out_keep, out_got, dq_keep, dq_got, out, dq):
@@ -210,7 +212,7 @@
 
 
 def backward(
-    plan, prob, stats_own, stats_mate, acc_in, q_cols, g_raw, kv_mine, kv_mate,
+    plan, prob, stats_own, stats_mate, acc_in, q_cols, g_raw, g_turned, kv_mine, kv_mate,
     out_keep, out_give, ds_out, dkv_keep, dkv_give,
     order, g_rows, ds_rows, delta_rows, g_cols, sems,
     *, tok, heads, dim, group,
@@ -246,7 +248,8 @@
         out[:, h] = (acc_in[r, :] * scale).astype(jnp.bfloat16)
     for j in range(2 * heads):
         r = slice(j * tok, (j + 1) * tok)
-        g_cols[:, r] = jnp.transpose(g_rows[r, :])
+        turned = g_turned[:, r].astype(jnp.float32) * scales[j : j + 1, :]
+        g_cols[:, r] = turned.astype(jnp.bfloat16)
     chunks = [slice(r, r + group) for r in range(0, 2 * half, group)]
 
     _, lower, own_span = unpack(plan, spans)
@@ -383,9 +386,9 @@
     rows = jax.ShapeDtypeStruct((2 * heads * tok, dim), jnp.bfloat16)
     return pl.pallas_call(
         functools.partial(prepare, tok=tok, heads=heads, dim=dim),
-        out_shape=(rows, rows),
+        out_shape=(rows, rows, jax.ShapeDtypeStruct((dim, 2 * heads * tok), jnp.bfloat16)),
         in_specs=[VMEM_SPEC] * 4,
-        out_specs=(VMEM_SPEC,) * 2,
+        out_specs=(VMEM_SPEC,) * 3,
         compiler_params=small_params(),
         cost_estimate=SHORT,
         name="prepare",
@@ -443,7 +446,7 @@
 
 
 def backward_call(
-    plan, prob, stats_own, stats_mate, acc, q_cols, g_raw, kv_mine, kv_mate, group=768
+    plan, prob, stats_own, stats_mate, acc, q_cols, g_raw, g_turned, kv_mine, kv_mate, group=768
 ):
     spans, tok, dim, heads, n_rows = sizes_of(g_raw, kv_mine)
     rows = jax.ShapeDtypeStruct((tok, heads * dim), jnp.bfloat16)
@@ -451,7 +454,7 @@
     return pl.pallas_call(
         functools.partial(backward, tok=tok, heads=heads, dim=dim, group=group),
         out_shape=(rows, rows, pltpu.HBM(prob.shape, jnp.bfloat16), part, part),
-        in_specs=[SMEM_SPEC] + [VMEM_SPEC] * 8,
+        in_specs=[SMEM_SPEC] + [VMEM_SPEC] * 9,
         out_specs=(VMEM_SPEC, VMEM_SPEC, HBM_SPEC, VMEM_SPEC, VMEM_SPEC),
         scratch_shapes=[
             pltpu.SMEM((spans,), jnp.int32),
@@ -463,7 +466,7 @@
         ],
         compiler_params=small_params(BACKWARD_LIMIT),
         name="attend_backward",
-    )(plan, prob, stats_own, stats_mate, acc, q_cols, g_raw, kv_mine, kv_mate)
+    )(plan, prob, stats_own, stats_mate, acc, q_cols, g_raw, g_turned, kv_mine, kv_mate)
 
 
 def finish_call(plan, ds_rows, kv_mine, kv_mate, side, cost):
@@ -526,7 +529,7 @@
     kv_out, own_squares = spread_call(key_states, value_states, queries, n_z)
     kv_mine = lax.all_to_all(kv_out, "z", 0, 0)
     square_sum = head_sum(row_squares_call(own_squares, q_mate))
-    q_raw, g_raw = prepare_call(queries, q_mate, out_grad, g_mate, dim)
+    q_raw, g_raw, g_turned = prepare_call(queries, q_mate, out_grad, g_mate, dim)
     kv_mine, square_sum, q_raw, g_raw = lax.optimization_barrier(
         (kv_mine, square_sum, q_raw, g_raw)
     )
@@ -536,7 +539,7 @@
     prob, acc, stats = forward_call(plan, q_rows, g_raw, kv_mine, kv_mate)
     stats_mate = lax.ppermute(stats, "xh", SWAP)
     out_keep, out_give, ds_rows, dkv_keep, dkv_give = backward_call(
-        plan, prob, stats, stats_mate, acc, q_cols, g_raw, kv_mine, kv_mate
+        plan, prob, stats, stats_mate, acc, q_cols, g_raw, g_turned, kv_mine, kv_mate
     )
     out_got = lax.ppermute(out_give, "xh", SWAP)
     dkv_got = lax.ppermute(dkv_give, "core", SWAP)

time: 73.5 us -> 73.6 us (level); the launches traced: 73.2 us -> 74.2 us
  starting transfers between devices: 31.2 us -> 34.3 us
  Pallas kernels: 16.3 us -> 13.4 us
  waiting for transfers between devices: 23.4 us -> 24.3 us
    all_to_all x1, starting transfers between devices: 4.54 us -> 7.61 us  [shards(): pieces = lax.all_to_all(chip, 'z', 0, 0)]
    pallas_call x1, Pallas kernels: 3.45 us -> 2.22 us  [forward_call(): pl.pallas_call(functools.partial(forward, tok=tok, heads=heads, dim=dim,...]
    pallas_call x2, Pallas kernels: 5.03 us -> 4.05 us  [finish_call(): pl.pallas_call(functools.partial(finish, tok=tok, heads=heads, dim=dim, f...]
    pallas_call x1, Pallas kernels: 3.68 us -> 2.83 us  [backward_call(): pl.pallas_call(functools.partial(backward, tok=tok, heads=heads, dim=dim,...]
  transfers between devices with their start and end apart: 13 -> 13, of which waited for: 9 -> 10; matrix products, arithmetic and copies ran while one was open for 0% -> 0% of each run, Pallas kernels for 11% -> 10%
where the time goes in v4:
time: 73.6 us; the launch traced here: 74.2 us
  starting transfers between devices  34.3 us (47%)
  waiting for transfers between devices  24.3 us (33%)
  Pallas kernels  13.4 us (18%)
  local copies, waits for them, and re-layouts  1.39 us (2%)
  between operations  0.75 us (1%)
    all_to_all x1, starting transfers between devices, shards(): kv_mine = lax.all_to_all(kv_out, 'z', 0, 0)  8.31 us
    all_to_all x1, starting transfers between devices, shards(): pieces = lax.all_to_all(chip, 'z', 0, 0)  7.61 us
    all_to_all x1, waiting for transfers between devices, shards(): kv_mine = lax.all_to_all(kv_out, 'z', 0, 0)  6.06 us
    all_to_all x1, waiting for transfers between devices, shards(): pieces = lax.all_to_all(chip, 'z', 0, 0)  5.32 us
    ppermute x1, waiting for transfers between devices, shards(): dq_got = lax.ppermute(dq_give, 'xh', SWAP)  4.55 us
    pallas_call x2, Pallas kernels, finish_call(): pl.pallas_call(functools.partial(finish, tok=tok, heads=heads, dim=dim, f...  4.05 us
    ppermute x3, starting transfers between devices, head_sum(): lax.ppermute(x, 'y', [(i, (i + d) % n) for i in range(n)])  3.77 us
    ppermute x1, starting transfers between devices, shards(): q_mate = lax.ppermute(queries, 'xh', SWAP)  3.66 us
  transfers between devices with their start and end apart: 13, of which 10 were waited for; matrix products, arithmetic and copies ran while one was open for 0% of the time, Pallas kernels for 10%

profile of v4, /device:TPU:1, one launch (start us, length us, event | category | flops | bytes accessed | tf_op | source)
XLA Modules:
  0.0 74.2 jit_solution(17301137630717948052)
XLA Ops:
  0.6 3.7 %collective-permute-start = (bf16[128,768]{1,0:T(8,128)(2,1)}, bf16[128,768]{1,0:T(8,128)(2,1)S(1)}, u32[]{:S(2)}, u32[]{:S(2)}) collective-permute-start(bf16[128,768]{1,0:T(8,128)(2,1)} %queries.3), channel_id=1, source_target_pairs={{0,16},{16,0},{1,17},{17,1},{2,18},{18,2},{3,19},{19,3},{4,20},{20... | collective-permute-start | bytes 589832 | tf_op jit(solution)/shard_map/ppermute | solution.py:527
  4.4 1.8 %spread.1 = (bf16[8,128,256]{2,1,0:T(8,128)(2,1)}, f32[1,128]{1,0:T(1,128)}) custom-call(bf16[128,128]{1,0:T(8,128)(2,1)} %keys.1, bf16[128,128]{1,0:T(8,128)(2,1)} %values.1, bf16[128,768]{1,0:T(8,128)(2,1)} %queries.3), custom_call_target="tpu_custom_call" | custom-call | tf_op jit(solution)/shard_map/spread/pallas_call | solution.py:498
  6.2 8.3 %all-to-all-start = ((bf16[8,128,256]{2,1,0:T(8,128)(2,1)}), bf16[8,128,256]{2,1,0:T(8,128)(2,1)S(1)}, u32[]{:S(2)}, u32[]{:S(2)}) async-start(bf16[8,128,256]{2,1,0:T(8,128)(2,1)} %get-tuple-element.28), calls=%async_computation | async-start | bytes 1048576 | tf_op jit(solution)/shard_map/all_to_all | solution.py:530
  14.6 0.6 copy-done.2
  15.4 1.3 %collective-permute-start.1 = (f32[2,128]{1,0:T(2,128)S(1)}, f32[2,128]{1,0:T(2,128)S(1)}, u32[]{:S(2)}, u32[]{:S(2)}) collective-permute-start(f32[2,128]{1,0:T(2,128)S(1)} %row_squares.1), channel_id=1, source_target_pairs={{0,1},{1,0},{2,3},{3,2},{4,5},{5,4},{6,7},{7,6},{8,9},{9,8},{10,11... | collective-permute-start | bytes 3080 | tf_op jit(solution)/shard_map/ppermute | solution.py:511
  16.7 1.2 %collective-permute-done.1 = f32[2,128]{1,0:T(2,128)S(1)} collective-permute-done((f32[2,128]{1,0:T(2,128)S(1)}, f32[2,128]{1,0:T(2,128)S(1)}, u32[]{:S(2)}, u32[]{:S(2)}) %collective-permute-start.1) | collective-permute-done | bytes 1056 | tf_op jit(solution)/shard_map/ppermute | solution.py:511
  17.9 2.7 %collective-permute-start.4 = (f32[2,128]{1,0:T(2,128)S(1)}, f32[2,128]{1,0:T(2,128)S(1)}, u32[]{:S(2)}, u32[]{:S(2)}) collective-permute-start(f32[2,128]{1,0:T(2,128)S(1)} %add.12), channel_id=1, source_target_pairs={{0,6},{2,0},{4,2},{6,4},{1,7},{3,1},{5,3},{7,5},{8,14},{10,8},{12,... | collective-permute-start | bytes 3080 | tf_op jit(solution)/shard_map/ppermute | solution.py:513
  20.6 0.3 collective-permute-start.3
  20.9 0.7 collective-permute-start.2
  21.7 0.2 prepare.1
  21.9 2.9 %collective-permute-done.3 = f32[2,128]{1,0:T(2,128)S(1)} collective-permute-done((f32[2,128]{1,0:T(2,128)S(1)}, f32[2,128]{1,0:T(2,128)S(1)}, u32[]{:S(2)}, u32[]{:S(2)}) %collective-permute-start.3) | collective-permute-done | bytes 1056 | tf_op jit(solution)/shard_map/ppermute | solution.py:513
  24.9 6.1 %all-to-all-done.kv_mine = bf16[8,128,256]{2,1,0:T(8,128)(2,1)S(1)} async-done(((bf16[8,128,256]{2,1,0:T(8,128)(2,1)}), bf16[8,128,256]{2,1,0:T(8,128)(2,1)S(1)}, u32[]{:S(2)}, u32[]{:S(2)}) %all-to-all-start) | async-done | bytes 524320 | tf_op jit(solution)/shard_map/all_to_all | solution.py:530
  30.9 2.0 %collective-permute-start.6 = (bf16[8,128,256]{2,1,0:T(8,128)(2,1)S(1)}, bf16[8,128,256]{2,1,0:T(8,128)(2,1)S(1)}, u32[]{:S(2)}, u32[]{:S(2)}) collective-permute-start(bf16[8,128,256]{2,1,0:T(8,128)(2,1)S(1)} %all-to-all-done.kv_mine), channel_id=1, source_target_pairs={{0,8},{8,0},{1,9},{9,1},{2,10},{10,2},{3,11},{11,3},{4,12},{12,4},... | collective-permute-start | bytes 1572872 | tf_op jit(solution)/shard_map/ppermute | solution.py:536
  33.1 0.4 normalize.1
  33.5 1.0 %collective-permute-done.6.kv_mate = bf16[8,128,256]{2,1,0:T(8,128)(2,1)S(1)} collective-permute-done((bf16[8,128,256]{2,1,0:T(8,128)(2,1)S(1)}, bf16[8,128,256]{2,1,0:T(8,128)(2,1)S(1)}, u32[]{:S(2)}, u32[]{:S(2)}) %collective-permute-start.6) | collective-permute-done | bytes 524320 | tf_op jit(solution)/shard_map/ppermute | solution.py:536
  34.5 2.2 %attend_forward.1 = (bf16[8,1536,256]{2,1,0:T(8,128)(2,1)S(1)}, f32[1536,128]{1,0:T(8,128)S(1)}, f32[48,128]{1,0:T(8,128)S(1)}) custom-call(s32[27]{0:T(128)S(1)} %concatenate.3.plan, bf16[1536,128]{1,0:T(8,128)(2,1)S(1)} %get-tuple-element.34.q_rows, bf16[1536,128]{1,0:T(8,128)(2,1)S(1)} %get-tuple-element.35.g_raw, ...), custom_call_target="tpu_custom_call" | custom-call | tf_op jit(solution)/shard_map/attend_forward/pallas_call | solution.py:428
  36.8 2.8 %collective-permute-start.7 = (f32[48,128]{1,0:T(8,128)S(1)}, f32[48,128]{1,0:T(8,128)S(1)}, u32[]{:S(2)}, u32[]{:S(2)}) collective-permute-start(f32[48,128]{1,0:T(8,128)S(1)} %get-tuple-element.38.stats_own), channel_id=1, source_target_pairs={{0,16},{16,0},{1,17},{17,1},{2,18},{18,2},{3,19},{19,3},{4,20},{20... | collective-permute-start | bytes 73736 | tf_op jit(solution)/shard_map/ppermute | solution.py:540
  39.5 1.4 %collective-permute-done.7.stats_mate = f32[48,128]{1,0:T(8,128)S(1)} collective-permute-done((f32[48,128]{1,0:T(8,128)S(1)}, f32[48,128]{1,0:T(8,128)S(1)}, u32[]{:S(2)}, u32[]{:S(2)}) %collective-permute-start.7) | collective-permute-done | bytes 24608 | tf_op jit(solution)/shard_map/ppermute | solution.py:540
  41.0 2.8 %attend_backward.1 = (bf16[128,768]{1,0:T(8,128)(2,1)S(1)}, bf16[128,768]{1,0:T(8,128)(2,1)S(1)}, bf16[8,1536,256]{2,1,0:T(8,128)(2,1)}, bf16[8,128,256]{2,1,0:T(8,128)(2,1)S(1)}, bf16[8,128,256]{2,1,0:T(8,128)(2,1)S(1)}) custom-call(s32[27]{0:T(128)S(1)} %concatenate.3.plan, bf16[8,1536,256]{2,1,0:T(8,128)(2,1)S(1)} %get-tuple-element.37.prob, ...), custom_call_target="tpu_custom_call" | custom-call | tf_op jit(solution)/shard_map/attend_backward/pallas_call | solution.py:454
  43.8 1.6 %collective-permute-start.9 = (bf16[8,128,256]{2,1,0:T(8,128)(2,1)S(1)}, bf16[8,128,256]{2,1,0:T(8,128)(2,1)S(1)}, u32[]{:S(2)}, u32[]{:S(2)}) collective-permute-start(bf16[8,128,256]{2,1,0:T(8,128)(2,1)S(1)} %get-tuple-element.45), channel_id=1, source_target_pairs={{0,8},{8,0},{1,9},{9,1},{2,10},{10,2},{3,11},{11,3},{4,12},{12,4},... | collective-permute-start | bytes 1572872 | tf_op jit(solution)/shard_map/ppermute | solution.py:545
  45.4 1.5 %collective-permute-done.9.other = bf16[8,128,256]{2,1,0:T(8,128)(2,1)S(1)} collective-permute-done((bf16[8,128,256]{2,1,0:T(8,128)(2,1)S(1)}, bf16[8,128,256]{2,1,0:T(8,128)(2,1)S(1)}, u32[]{:S(2)}, u32[]{:S(2)}) %collective-permute-start.9) | collective-permute-done | bytes 524320 | tf_op jit(solution)/shard_map/ppermute | solution.py:545
  47.0 0.9 %add_pair.1 = bf16[8,128,256]{2,1,0:T(8,128)(2,1)} custom-call(bf16[8,128,256]{2,1,0:T(8,128)(2,1)S(1)} %get-tuple-element.44.one, bf16[8,128,256]{2,1,0:T(8,128)(2,1)S(1)} %collective-permute-done.9.other), custom_call_target="tpu_custom_call" | custom-call | tf_op jit(solution)/shard_map/add_pair/pallas_call | solution.py:403
  47.9 7.6 %all-to-all-start.1 = ((bf16[8,128,256]{2,1,0:T(8,128)(2,1)}), bf16[8,128,256]{2,1,0:T(8,128)(2,1)S(1)}, u32[]{:S(2)}, u32[]{:S(2)}) async-start(bf16[8,128,256]{2,1,0:T(8,128)(2,1)} %add_pair.1), calls=%async_computation.1 | async-start | bytes 1048576 | tf_op jit(solution)/shard_map/all_to_all | solution.py:548
  55.5 2.7 %collective-permute-start.8 = (bf16[128,768]{1,0:T(8,128)(2,1)S(1)}, bf16[128,768]{1,0:T(8,128)(2,1)S(1)}, u32[]{:S(2)}, u32[]{:S(2)}) collective-permute-start(bf16[128,768]{1,0:T(8,128)(2,1)S(1)} %get-tuple-element.43), channel_id=1, source_target_pairs={{0,16},{16,0},{1,17},{17,1},{2,18},{18,2},{3,19},{19,3},{4,20},{20... | collective-permute-start | bytes 589832 | tf_op jit(solution)/shard_map/ppermute | solution.py:544
  58.3 2.0 %finish_mate.1 = bf16[128,768]{1,0:T(8,128)(2,1)S(1)} custom-call(s32[27]{0:T(128)S(1)} %concatenate.3.plan, bf16[8,1536,256]{2,1,0:T(8,128)(2,1)} %get-tuple-element.48.ds_in, bf16[8,128,256]{2,1,0:T(8,128)(2,1)S(1)} %all-to-all-done.kv_mine, bf16[8,128,256]{2,1,0:T(8,128)(2,1)S(1)} %collective-permute-done.6.kv_mate), custom_call_target="tpu_custom_call" | custom-call | flops 3000000000 | bytes 1024 | tf_op jit(solution)/shard_map/finish_mate/pallas_call | solution.py:479
  60.3 0.3 collective-permute-start.10
  60.6 2.0 %finish_own.1.dq_keep = bf16[128,768]{1,0:T(8,128)(2,1)S(1)} custom-call(s32[27]{0:T(128)S(1)} %concatenate.3.plan, bf16[8,1536,256]{2,1,0:T(8,128)(2,1)} %get-tuple-element.48.ds_in, bf16[8,128,256]{2,1,0:T(8,128)(2,1)S(1)} %all-to-all-done.kv_mine, bf16[8,128,256]{2,1,0:T(8,128)(2,1)S(1)} %collective-permute-done.6.kv_mate), custom_call_target="tpu_custom_call" | custom-call | flops 3000000000 | bytes 1024 | tf_op jit(solution)/shard_map/finish_own/pallas_call | solution.py:479
  62.6 0.2 collective-permute-done.8.out_got
  62.8 4.5 %collective-permute-done.10.dq_got = bf16[128,768]{1,0:T(8,128)(2,1)S(1)} collective-permute-done((bf16[128,768]{1,0:T(8,128)(2,1)S(1)}, bf16[128,768]{1,0:T(8,128)(2,1)S(1)}, u32[]{:S(2)}, u32[]{:S(2)}) %collective-permute-start.10) | collective-permute-done | bytes 196640 | tf_op jit(solution)/shard_map/ppermute | solution.py:550
  67.4 0.8 %merge.1 = (bf16[128,768]{1,0:T(8,128)(2,1)}, bf16[128,768]{1,0:T(8,128)(2,1)}) custom-call(bf16[128,768]{1,0:T(8,128)(2,1)S(1)} %get-tuple-element.42.out_keep, bf16[128,768]{1,0:T(8,128)(2,1)S(1)} %collective-permute-done.8.out_got, bf16[128,768]{1,0:T(8,128)(2,1)S(1)} %finish_own.1.dq_keep, bf16[128,768]{1,0:T(8,128)(2,1)S(1)} %collective-permute-done.10.dq_got), custom_call_target="tpu_custom_call" | custom-call | flops 1024 | bytes 1024 | tf_op jit(solution)/shard_map/merge/pallas_call | solution.py:415
  68.2 5.3 %all-to-all-done.1 = bf16[8,128,256]{2,1,0:T(8,128)(2,1)S(1)} async-done(((bf16[8,128,256]{2,1,0:T(8,128)(2,1)}), bf16[8,128,256]{2,1,0:T(8,128)(2,1)S(1)}, u32[]{:S(2)}, u32[]{:S(2)}) %all-to-all-start.1) | async-done | bytes 524320 | tf_op jit(solution)/shard_map/all_to_all | solution.py:548
  73.6 0.6 fusion
  (24 shorter events, 0.5 us)
Async XLA Ops:
  0.6 13.9 %collective-permute-start = (bf16[128,768]{1,0:T(8,128)(2,1)}, bf16[128,768]{1,0:T(8,128)(2,1)S(1)}, u32[]{:S(2)}, u32[]{:S(2)}) collective-permute-start(bf16[128,768]{1,0:T(8,128)(2,1)} %queries.3), channel_id=1, source_target_pairs={{0,16},{16,0},{1,17},{17,1},{2,18},{18,2},{3,19},{19,3},{4,20},{20... | collective-permute-start | bytes 589832 | tf_op jit(solution)/shard_map/ppermute | solution.py:527
  4.3 17.4 %collective-permute-start.5 = (bf16[128,768]{1,0:T(8,128)(2,1)}, bf16[128,768]{1,0:T(8,128)(2,1)S(1)}, u32[]{:S(2)}, u32[]{:S(2)}) collective-permute-start(bf16[128,768]{1,0:T(8,128)(2,1)} %out_grad.1), channel_id=1, source_target_pairs={{0,16},{16,0},{1,17},{17,1},{2,18},{18,2},{3,19},{19,3},{4,20},{20... | collective-permute-start | bytes 589832 | tf_op jit(solution)/shard_map/ppermute | solution.py:528
  6.2 24.7 %all-to-all-start = ((bf16[8,128,256]{2,1,0:T(8,128)(2,1)}), bf16[8,128,256]{2,1,0:T(8,128)(2,1)S(1)}, u32[]{:S(2)}, u32[]{:S(2)}) async-start(bf16[8,128,256]{2,1,0:T(8,128)(2,1)} %get-tuple-element.28), calls=%async_computation | async-start | bytes 1048576 | tf_op jit(solution)/shard_map/all_to_all | solution.py:530
  14.5 0.7 copy-start.2
  15.2 6.4 %copy-start = (bf16[128,768]{1,0:T(8,128)(2,1)S(1)}, bf16[128,768]{1,0:T(8,128)(2,1)}, u32[]{:S(2)}) copy-start(bf16[128,768]{1,0:T(8,128)(2,1)} %queries.3) | copy-start | bytes 589828
  15.2 6.4 %copy-start.1 = (bf16[128,768]{1,0:T(8,128)(2,1)S(1)}, bf16[128,768]{1,0:T(8,128)(2,1)}, u32[]{:S(2)}) copy-start(bf16[128,768]{1,0:T(8,128)(2,1)} %out_grad.1) | copy-start | bytes 589828
  15.2 17.8 %copy-start.3 = (f32[768]{0:T(1024)S(1)}, f32[768]{0:T(1024)}, u32[]{:S(2)}) copy-start(f32[768]{0:T(1024)} %param.12) | copy-start | bytes 9220
  15.2 17.8 %copy-start.4 = (s32[8]{0:T(128)S(1)}, s32[8]{0:T(128)}, u32[]{:S(2)}) copy-start(s32[8]{0:T(128)} %param.13) | copy-start | bytes 100
  15.2 17.8 %copy-start.5 = (s32[8]{0:T(128)S(1)}, s32[8]{0:T(128)}, u32[]{:S(2)}) copy-start(s32[8]{0:T(128)} %param.14) | copy-start | bytes 100
  15.2 17.8 %copy-start.6 = (s32[8]{0:T(128)S(1)}, s32[8]{0:T(128)}, u32[]{:S(2)}) copy-start(s32[8]{0:T(128)} %param.15) | copy-start | bytes 100
  15.4 2.5 %collective-permute-start.1 = (f32[2,128]{1,0:T(2,128)S(1)}, f32[2,128]{1,0:T(2,128)S(1)}, u32[]{:S(2)}, u32[]{:S(2)}) collective-permute-start(f32[2,128]{1,0:T(2,128)S(1)} %row_squares.1), channel_id=1, source_target_pairs={{0,1},{1,0},{2,3},{3,2},{4,5},{5,4},{6,7},{7,6},{8,9},{9,8},{10,11... | collective-permute-start | bytes 3080 | tf_op jit(solution)/shard_map/ppermute | solution.py:511
  17.9 4.0 %collective-permute-start.4 = (f32[2,128]{1,0:T(2,128)S(1)}, f32[2,128]{1,0:T(2,128)S(1)}, u32[]{:S(2)}, u32[]{:S(2)}) collective-permute-start(f32[2,128]{1,0:T(2,128)S(1)} %add.12), channel_id=1, source_target_pairs={{0,6},{2,0},{4,2},{6,4},{1,7},{3,1},{5,3},{7,5},{8,14},{10,8},{12,... | collective-permute-start | bytes 3080 | tf_op jit(solution)/shard_map/ppermute | solution.py:513
  20.6 4.2 %collective-permute-start.3 = (f32[2,128]{1,0:T(2,128)S(1)}, f32[2,128]{1,0:T(2,128)S(1)}, u32[]{:S(2)}, u32[]{:S(2)}) collective-permute-start(f32[2,128]{1,0:T(2,128)S(1)} %add.12), channel_id=1, source_target_pairs={{0,4},{2,6},{4,0},{6,2},{1,5},{3,7},{5,1},{7,3},{8,12},{10,14},{12... | collective-permute-start | bytes 3080 | tf_op jit(solution)/shard_map/ppermute | solution.py:513
  20.9 3.9 %collective-permute-start.2 = (f32[2,128]{1,0:T(2,128)S(1)}, f32[2,128]{1,0:T(2,128)S(1)}, u32[]{:S(2)}, u32[]{:S(2)}) collective-permute-start(f32[2,128]{1,0:T(2,128)S(1)} %add.12), channel_id=1, source_target_pairs={{0,2},{2,4},{4,6},{6,0},{1,3},{3,5},{5,7},{7,1},{8,10},{10,12},{12... | collective-permute-start | bytes 3080 | tf_op jit(solution)/shard_map/ppermute | solution.py:513
  30.9 3.6 %collective-permute-start.6 = (bf16[8,128,256]{2,1,0:T(8,128)(2,1)S(1)}, bf16[8,128,256]{2,1,0:T(8,128)(2,1)S(1)}, u32[]{:S(2)}, u32[]{:S(2)}) collective-permute-start(bf16[8,128,256]{2,1,0:T(8,128)(2,1)S(1)} %all-to-all-done.kv_mine), channel_id=1, source_target_pairs={{0,8},{8,0},{1,9},{9,1},{2,10},{10,2},{3,11},{11,3},{4,12},{12,4},... | collective-permute-start | bytes 1572872 | tf_op jit(solution)/shard_map/ppermute | solution.py:536
  36.8 4.2 %collective-permute-start.7 = (f32[48,128]{1,0:T(8,128)S(1)}, f32[48,128]{1,0:T(8,128)S(1)}, u32[]{:S(2)}, u32[]{:S(2)}) collective-permute-start(f32[48,128]{1,0:T(8,128)S(1)} %get-tuple-element.38.stats_own), channel_id=1, source_target_pairs={{0,16},{16,0},{1,17},{17,1},{2,18},{18,2},{3,19},{19,3},{4,20},{20... | collective-permute-start | bytes 73736 | tf_op jit(solution)/shard_map/ppermute | solution.py:540
  43.8 3.2 %collective-permute-start.9 = (bf16[8,128,256]{2,1,0:T(8,128)(2,1)S(1)}, bf16[8,128,256]{2,1,0:T(8,128)(2,1)S(1)}, u32[]{:S(2)}, u32[]{:S(2)}) collective-permute-start(bf16[8,128,256]{2,1,0:T(8,128)(2,1)S(1)} %get-tuple-element.45), channel_id=1, source_target_pairs={{0,8},{8,0},{1,9},{9,1},{2,10},{10,2},{3,11},{11,3},{4,12},{12,4},... | collective-permute-start | bytes 1572872 | tf_op jit(solution)/shard_map/ppermute | solution.py:545
  47.9 25.6 %all-to-all-start.1 = ((bf16[8,128,256]{2,1,0:T(8,128)(2,1)}), bf16[8,128,256]{2,1,0:T(8,128)(2,1)S(1)}, u32[]{:S(2)}, u32[]{:S(2)}) async-start(bf16[8,128,256]{2,1,0:T(8,128)(2,1)} %add_pair.1), calls=%async_computation.1 | async-start | bytes 1048576 | tf_op jit(solution)/shard_map/all_to_all | solution.py:548
  55.5 7.3 %collective-permute-start.8 = (bf16[128,768]{1,0:T(8,128)(2,1)S(1)}, bf16[128,768]{1,0:T(8,128)(2,1)S(1)}, u32[]{:S(2)}, u32[]{:S(2)}) collective-permute-start(bf16[128,768]{1,0:T(8,128)(2,1)S(1)} %get-tuple-element.43), channel_id=1, source_target_pairs={{0,16},{16,0},{1,17},{17,1},{2,18},{18,2},{3,19},{19,3},{4,20},{20... | collective-permute-start | bytes 589832 | tf_op jit(solution)/shard_map/ppermute | solution.py:544
  60.3 7.1 %collective-permute-start.10 = (bf16[128,768]{1,0:T(8,128)(2,1)S(1)}, bf16[128,768]{1,0:T(8,128)(2,1)S(1)}, u32[]{:S(2)}, u32[]{:S(2)}) collective-permute-start(bf16[128,768]{1,0:T(8,128)(2,1)S(1)} %finish_mate.1), channel_id=1, source_target_pairs={{0,16},{16,0},{1,17},{17,1},{2,18},{18,2},{3,19},{19,3},{4,20},{20... | collective-permute-start | bytes 589832 | tf_op jit(solution)/shard_map/ppermute | solution.py:550
